TPU v7x, 32 devices: a whole 2x2x4 slice. The times are simulated.
32 devices in a mesh: ia: 4 (over z), ja: 4 (over x, core), ka: 2 (over y).
Axes of the slice: x: 2, y: 2, z: 4, core: 2. Of those that a mesh axis runs over, the one named last changes fastest.
Arguments:
- tensor: float32 [512, 256, 512], P('ia', 'ja', 'ka'), may hold values from -6 to 6
- factor_b: float32 [4, 64, 256], P('ja', ('ia', 'ka')), may hold values from -0.375 to 0.375
- factor_c: float32 [2, 256, 256], P('ka', ('ia', 'ja')), may hold values from -0.25 to 0.25
Outputs:
- new_a: float32 [4, 128, 256], P('ia', ('ja', 'ka'))
- new_b: float32 [4, 64, 256], P('ja', ('ia', 'ka'))
- new_c: float32 [2, 256, 256], P('ka', ('ia', 'ja'))
All inputs are finite; a program needn't handle non-finite values.
Results may differ from a plain program's by a relative error of at most 0.00011.
Values sent between devices are 32-bit elements; how exact they have to be, the bound alone decides.
No kernel may reach another device: no remote copies, remote signals or barrier semaphores. Data moves between devices by JAX's collectives and lax.ppermute only.
A program may use at most 64 MiB of HBM per device.

v0:
```python
import jax
import jax.numpy as jnp
from jax import lax
from jax.sharding import PartitionSpec as P

HIGH = lax.Precision.HIGHEST


def gram_of(rows):
    return jnp.dot(rows.T, rows, precision=HIGH, preferred_element_type=jnp.float32)


def solve_rows(right, gram):
    factor = jnp.linalg.cholesky(gram)
    return jax.scipy.linalg.cho_solve((factor, True), right.T).T


def on_device(tensor, factor_b, factor_c):
    i_dev, j_dev, k_dev = tensor.shape
    b_slice = lax.all_gather(factor_b, ("ia", "ka"), axis=1, tiled=True)[0]
    c_slice = lax.all_gather(factor_c, ("ia", "ja"), axis=1, tiled=True)[0]
    gram_b, gram_c = lax.psum((gram_of(factor_b[0]), gram_of(factor_c[0])), ("ia", "ja", "ka"))
    partial_t = jnp.einsum("ijk,kr->ijr", tensor, c_slice, precision=HIGH)
    partial_a = jnp.einsum("ijr,jr->ir", partial_t, b_slice, precision=HIGH)
    mttkrp_a = lax.psum_scatter(partial_a, ("ja", "ka"), scatter_dimension=0, tiled=True)
    new_a = solve_rows(mttkrp_a, gram_b * gram_c)
    a_slice = lax.all_gather(new_a[None], ("ja", "ka"), axis=1, tiled=True)[0]
    gram_a = lax.psum(gram_of(new_a), ("ia", "ja", "ka"))
    inner = jnp.einsum("ijk,ir->jkr", tensor, a_slice, precision=HIGH)
    partial_b = jnp.einsum("jkr,kr->jr", inner, c_slice, precision=HIGH)
    mttkrp_b = lax.psum_scatter(partial_b, ("ia", "ka"), scatter_dimension=0, tiled=True)
    new_b = solve_rows(mttkrp_b, gram_a * gram_c)
    b_new_slice = lax.all_gather(new_b[None], ("ia", "ka"), axis=1, tiled=True)[0]
    gram_b_new = lax.psum(gram_of(new_b), ("ia", "ja", "ka"))
    weights = (a_slice[:, None, :] * b_new_slice[None, :, :]).reshape(i_dev * j_dev, -1)
    flat = tensor.reshape(i_dev * j_dev, k_dev)
    partial_c = jnp.einsum("ak,ar->kr", flat, weights, precision=HIGH)
    mttkrp_c = lax.psum_scatter(partial_c, ("ia", "ja"), scatter_dimension=0, tiled=True)
    new_c = solve_rows(mttkrp_c, gram_a * gram_b_new)
    return (new_a[None], new_b[None], new_c[None])


def solution(mesh):
    return jax.shard_map(
        on_device,
        mesh=mesh,
        in_specs=(P("ia", "ja", "ka"), P("ja", ("ia", "ka"), None), P("ka", ("ia", "ja"), None)),
        out_specs=(
            P("ia", ("ja", "ka"), None),
            P("ja", ("ia", "ka"), None),
            P("ka", ("ia", "ja"), None),
        ),
        check_vma=False,
    )
```

profile of v0, /device:TPU:0, one launch (start us, length us, event | category | flops | bytes accessed | tf_op | source)
XLA Modules:
  0.0 725.0 jit_solution(13259686135649260689)
XLA Ops:
  8.1 32.5 %all_gather.13 = f32[1,64,256]{2,1,0:T(8,128)S(1)} all-gather(f32[1,8,256]{2,1,0:T(8,128)} %param.7), channel_id=1, replica_groups=mesh['ia'=4,'ja'=4,'ka'=2] {'ia','ka'}, dimensions={1}, use_global_device_ids=true | all-gather | bytes 73728 | tf_op jit(solution)/shard_map/all_gather | solution.py:20
  40.6 19.5 %all_gather.12 = f32[1,256,256]{2,1,0:T(8,128)S(1)} all-gather(f32[1,16,256]{2,1,0:T(8,128)} %param.8), channel_id=1, replica_groups=mesh['ia'=4,'ja'=4,'ka'=2] {'ia','ja'}, dimensions={1}, use_global_device_ids=true | all-gather | bytes 278528 | tf_op jit(solution)/shard_map/all_gather | solution.py:21
  60.1 9.7 %multiply_reduce_fusion = f32[256,128]{0,1:T(8,128)} fusion(f32[256,64]{0,1:T(8,128)S(1)} %bitcast.170, f32[128,64,256]{2,1,0:T(8,128)} %param.6, f32[1,256,256]{2,1,0:T(8,128)S(1)} %all_gather.12), kind=kOutput, calls=%fused_computation.9 | convolution fusion | flops 6446612480 | bytes 8847360 | tf_op jit(solution)/shard_map/ijk,kr->ijr/dot_general | solution.py:23
  72.6 30.8 %reduce-scatter.10.cloned.1.call-done = f32[16,256]{1,0:T(8,128)} async-done(((f32[128,256]{1,0:T(8,128)}), f32[16,256]{1,0:T(8,128)}) %reduce-scatter.10.cloned.1.call-update) | async-done | bytes 16400
  104.2 100.2 %all-reduce.10.cloned.1.call-done = (f32[256,256]{0,1:T(8,128)}, f32[256,256]{0,1:T(8,128)}) async-done(((f32[256,256]{0,1:T(8,128)}, f32[256,256]{0,1:T(8,128)}), (f32[256,256]{0,1:T(8,128)}, f32[256,256]{0,1:T(8,128)})) %all-reduce.10.cloned.1.call-update) | async-done | bytes 524304 | tf_op jit(solution)/shard_map/psum | solution.py:22
  205.7 11.7 %cholesky.172 = f32[128,128]{1,0:T(8,128)S(1)} custom-call(f32[128,128]{1,0:T(8,128)S(1)} %cholesky.270), custom_call_target="Cholesky" | custom-call | tf_op jit(solution)/shard_map/jit(cholesky)/cholesky | solution.py:14
  217.5 9.8 %custom-call.24 = f32[1,128,128]{1,2,0:T(8,128)S(1)} custom-call(f32[1,128,128]{2,1,0:T(8,128)S(1)} %get-tuple-element.72), custom_call_target="InvertDiagBlocksLowerTriangular" | custom-call | tf_op jit(solution)/shard_map/jit(cholesky)/cholesky | solution.py:14
  227.8 11.7 %cholesky.189 = f32[128,128]{1,0:T(8,128)S(1)} custom-call(f32[128,128]{1,0:T(8,128)S(1)} %convolution_subtract_fusion.5), custom_call_target="Cholesky" | custom-call | tf_op jit(solution)/shard_map/jit(cholesky)/cholesky | solution.py:14
  245.8 19.7 %custom-call.25 = f32[2,128,128]{1,2,0:T(8,128)S(1)} custom-call(f32[2,128,128]{2,1,0:T(8,128)S(1)} %get-tuple-element.27), custom_call_target="InvertDiagBlocksLowerTriangular" | custom-call | tf_op jit(solution)/shard_map/jit(_cho_solve)/triangular_solve | solution.py:15
  268.6 16.4 %all-gather = f32[128,256]{1,0:T(8,128)S(1)} all-gather(f32[16,256]{1,0:T(8,128)S(1)} %get-tuple-element.73), channel_id=2, replica_groups=mesh['ia'=4,'ja'=4,'ka'=2] {'ja','ka'}, dimensions={0}, use_global_device_ids=true | all-gather | bytes 147456 | tf_op jit(solution)/shard_map/all_gather | solution.py:27
  285.0 24.3 %fusion.5 = f32[256,64,256]{2,0,1:T(8,128)} fusion(f32[128,64,256]{2,1,0:T(8,128)} %param.6, f32[128,256]{1,0:T(8,128)S(1)} %all-gather), kind=kOutput, calls=%fused_computation.12 | convolution fusion | flops 6442450944 | bytes 25296896 | tf_op jit(solution)/shard_map/ijk,ir->jkr/dot_general | solution.py:29
  309.4 27.7 %fusion = f32[256,1,64]{2,1,0:T(1,128)S(1)} fusion(f32[256,256,1]{0,2,1:T(1,128)S(1)} %copy.35, f32[256,64,256]{2,0,1:T(8,128)} %fusion.5), kind=kOutput, calls=%fused_computation.6 | convolution fusion | flops 50331648 | bytes 17104896 | tf_op jit(solution)/shard_map/jkr,kr->jr/dot_general | solution.py:30
  338.1 95.0 %all-reduce.6.cloned.1.call-done = f32[256,256]{0,1:T(8,128)} async-done(((f32[256,256]{0,1:T(8,128)}), f32[256,256]{0,1:T(8,128)}) %all-reduce.6.cloned.1.call-update) | async-done | bytes 262160 | tf_op jit(solution)/shard_map/psum | solution.py:28
  434.3 11.7 %cholesky.206 = f32[128,128]{1,0:T(8,128)S(1)} custom-call(f32[128,128]{1,0:T(8,128)S(1)} %cholesky.273), custom_call_target="Cholesky" | custom-call | tf_op jit(solution)/shard_map/jit(cholesky)/cholesky | solution.py:14
  446.1 9.8 %custom-call.26 = f32[1,128,128]{1,2,0:T(8,128)S(1)} custom-call(f32[1,128,128]{2,1,0:T(8,128)S(1)} %get-tuple-element.68), custom_call_target="InvertDiagBlocksLowerTriangular" | custom-call | tf_op jit(solution)/shard_map/jit(cholesky)/cholesky | solution.py:14
  456.4 11.7 %cholesky.223 = f32[128,128]{1,0:T(8,128)S(1)} custom-call(f32[128,128]{1,0:T(8,128)S(1)} %convolution_subtract_fusion.3), custom_call_target="Cholesky" | custom-call | tf_op jit(solution)/shard_map/jit(cholesky)/cholesky | solution.py:14
  474.8 19.7 %custom-call.20 = f32[2,128,128]{1,2,0:T(8,128)S(1)} custom-call(f32[2,128,128]{2,1,0:T(8,128)S(1)} %get-tuple-element.20), custom_call_target="InvertDiagBlocksLowerTriangular" | custom-call | tf_op jit(solution)/shard_map/jit(_cho_solve)/triangular_solve | solution.py:15
  498.4 30.5 %all-gather.1 = f32[64,256]{1,0:T(8,128)S(1)} all-gather(f32[8,256]{1,0:T(8,128)S(1)} %get-tuple-element.75), channel_id=3, replica_groups=mesh['ia'=4,'ja'=4,'ka'=2] {'ia','ka'}, dimensions={0}, use_global_device_ids=true | all-gather | bytes 73728 | tf_op jit(solution)/shard_map/all_gather | solution.py:33
  529.4 14.3 %fusion.10 = f32[256,256]{0,1:T(8,128)S(1)} fusion(f32[128,64,256]{2,1,0:T(8,128)} %param.6, f32[64,256]{1,0:T(8,128)S(1)} %all-gather.1, f32[128,256]{0,1:T(8,128)S(1)} %copy.22), kind=kOutput, calls=%fused_computation.17 | convolution fusion | flops 6444548096 | bytes 8847360 | tf_op jit(solution)/shard_map/ak,ar->kr/dot_general | solution.py:37
  544.5 108.2 %all-reduce.8.cloned.1.call-done = f32[256,256]{0,1:T(8,128)} async-done(((f32[256,256]{0,1:T(8,128)}), f32[256,256]{0,1:T(8,128)}) %all-reduce.8.cloned.1.call-update) | async-done | bytes 262160 | tf_op jit(solution)/shard_map/psum | solution.py:34
  654.0 11.9 %cholesky.240 = f32[128,128]{1,0:T(8,128)S(1)} custom-call(f32[128,128]{1,0:T(8,128)S(1)} %cholesky.276), custom_call_target="Cholesky" | custom-call | tf_op jit(solution)/shard_map/jit(cholesky)/cholesky | solution.py:14
  665.9 9.8 %custom-call.27 = f32[1,128,128]{1,2,0:T(8,128)S(1)} custom-call(f32[1,128,128]{2,1,0:T(8,128)S(1)} %get-tuple-element.64), custom_call_target="InvertDiagBlocksLowerTriangular" | custom-call | tf_op jit(solution)/shard_map/jit(cholesky)/cholesky | solution.py:14
  676.2 11.7 %cholesky.257 = f32[128,128]{1,0:T(8,128)S(1)} custom-call(f32[128,128]{1,0:T(8,128)S(1)} %convolution_subtract_fusion.1), custom_call_target="Cholesky" | custom-call | tf_op jit(solution)/shard_map/jit(cholesky)/cholesky | solution.py:14
  694.9 19.7 %custom-call.28 = f32[2,128,128]{1,2,0:T(8,128)S(1)} custom-call(f32[2,128,128]{2,1,0:T(8,128)S(1)} %get-tuple-element.28), custom_call_target="InvertDiagBlocksLowerTriangular" | custom-call | tf_op jit(solution)/shard_map/jit(_cho_solve)/triangular_solve | solution.py:15
  (115 shorter events, 48.7 us)
Async XLA Ops:
  8.0 63.0 %copy-start.3 = (f32[1,8,256]{2,1,0:T(8,128)S(1)}, f32[1,8,256]{2,1,0:T(8,128)}, u32[]{:S(2)}) copy-start(f32[1,8,256]{2,1,0:T(8,128)} %param.7) | copy-start | bytes 24580
  8.0 61.9 %copy-start.2 = (f32[1,16,256]{2,1,0:T(8,128)S(1)}, f32[1,16,256]{2,1,0:T(8,128)}, u32[]{:S(2)}) copy-start(f32[1,16,256]{2,1,0:T(8,128)} %param.8) | copy-start | bytes 49156
  8.0 95.4 %reduce-scatter.10.cloned.1.call-start = ((), (), s32[]{:S(2)}) async-start(), calls=%async_computation.5 | async-start | bytes 147456
  69.9 134.6 %all-reduce.10.cloned.1.call-start = ((), (), s32[]{:S(2)}) async-start(), calls=%async_computation.8 | async-start | bytes 1048576 | tf_op jit(solution)/shard_map/psum | solution.py:22
  72.2 360.9 %all-reduce.6.cloned.1.call-start = ((), (), s32[]{:S(2)}) async-start(), calls=%async_computation.3 | async-start | bytes 524288 | tf_op jit(solution)/shard_map/psum | solution.py:28
  309.4 123.7 %copy-start = (f32[256,256]{0,1:T(8,128)S(1)}, f32[256,256]{0,1:T(8,128)}, u32[]{:S(2)}) copy-start(f32[256,256]{0,1:T(8,128)} %get-tuple-element.54) | copy-start | bytes 786436
  309.4 185.1 %reduce-scatter.12.cloned.1.call-start = ((), (), s32[]{:S(2)}) async-start(), calls=%async_computation.6 | async-start | bytes 73728
  338.0 314.8 %all-reduce.8.cloned.1.call-start = ((), (), s32[]{:S(2)}) async-start(), calls=%async_computation.4 | async-start | bytes 524288 | tf_op jit(solution)/shard_map/psum | solution.py:34
  433.1 219.7 %copy-start.1 = (f32[256,256]{0,1:T(8,128)S(1)}, f32[256,256]{0,1:T(8,128)}, u32[]{:S(2)}) copy-start(f32[256,256]{0,1:T(8,128)} %all-reduce.6.cloned.1.call-done) | copy-start | bytes 786436
  529.0 185.6 %reduce-scatter.14.cloned.1.call-start = ((), (), s32[]{:S(2)}) async-start(), calls=%async_computation.7 | async-start | bytes 278528
Sparse Core Ops, SparseCore 0:
  70.0 33.4 reduce-scatter.9
  338.1 60.2 reduce-scatter.11
  544.6 54.3 reduce-scatter.13
Sparse Core Ops, SparseCore 1:
  76.7 127.7 all-reduce.9
  309.5 123.6 all-reduce.5
  529.0 123.7 all-reduce.7
where the time goes:
time: 730 us; the launch traced here: 725 us
  waiting for transfers between devices  334 us (46%)
  other arithmetic  168 us (23%)
  blocking collectives  98.9 us (14%)
  matrix products  86 us (12%)
  between operations  19.8 us (3%)
  local copies, waits for them, and re-layouts  16.5 us (2%)
    psum x1, waiting for transfers between devices, on_device(): gram_b_new = lax.psum(gram_of(new_b), ('ia', 'ja', 'ka'))  108 us
    another operation x20, other arithmetic, solve_rows(): factor = jnp.linalg.cholesky(gram)  103 us
    psum x1, waiting for transfers between devices, on_device(): lax.psum((gram_of(factor_b[0]), gram_of(factor_c[0])), ('ia', 'ja', 'ka'))  100 us
    psum x1, waiting for transfers between devices, on_device(): gram_a = lax.psum(gram_of(new_a), ('ia', 'ja', 'ka'))  95 us
    another operation x7, other arithmetic, solve_rows(): return jax.scipy.linalg.cho_solve((factor, True), right.T).T  59.1 us
    all_gather x1, blocking collectives, on_device(): b_slice = lax.all_gather(factor_b, ('ia', 'ka'), axis=1, tiled=True)[0]  32.5 us
    unnamed x9, waiting for transfers between devices  31 us
    all_gather x1, blocking collectives, on_device(): lax.all_gather(new_b[None], ('ia', 'ka'), axis=1, tiled=True)[0]  30.5 us
  transfers between devices with their start and end apart: 6, of which 4 were waited for; matrix products, arithmetic and copies ran while one was open for 23% of the time, Pallas kernels for 0%

commit v1 on v0

v1 whole, which is shorter than its diff:
```python
import functools

import jax
import jax.numpy as jnp
from jax import lax
from jax.experimental import pallas as pl
from jax.experimental.pallas import tpu as pltpu
from jax.sharding import PartitionSpec as P

HIGH = lax.Precision.HIGHEST
F32 = jnp.float32
BF16 = jnp.bfloat16
VMEM_LIMIT = 28 * 1024 * 1024
NN = (((1,), (0,)), ((), ()))
NT = (((1,), (1,)), ((), ()))
TN = (((0,), (0,)), ((), ()))


def mul(left, right, dims=NN):
    return lax.dot_general(left, right, dims, precision=HIGH, preferred_element_type=F32)


def split(value):
    high = value.astype(BF16)
    return high, (value - high.astype(F32)).astype(BF16)


def tree(values):
    values = list(values)
    while len(values) > 1:
        values = [a + b for a, b in zip(values[::2], values[1::2])]
    return values[0]


def bits(axis, count):
    assert count & (count - 1) == 0
    return [(axis, 1 << at) for at in reversed(range(count.bit_length() - 1))]


def swap(value, axis, distance):
    return lax.ppermute(value, axis, [(rank, rank ^ distance) for rank in range(lax.axis_size(axis))])


def grow(block, stages):
    for axis, distance in stages:
        block = jnp.concatenate([block, swap(block, axis, distance)], axis=0)
    return block


def origin(place, stages):
    masks = {}
    for at, (axis, distance) in enumerate(stages):
        masks[axis] = masks.get(axis, 0) ^ (distance if place >> at & 1 else 0)
    return masks


def invert_half(ref, which):
    size = 128
    count = size // 8
    lane = lax.broadcasted_iota(jnp.int32, (8, size), 1)
    sub = lax.broadcasted_iota(jnp.int32, (8, size), 0)
    rows = [ref[which, 8 * at : 8 * at + 8, :] for at in range(count)]

    def over_lanes(value, at):
        return jnp.broadcast_to(value[:, at : at + 1], (8, size))

    def over_rows(value, at):
        return jnp.broadcast_to(value[at : at + 1, :], (8, size))

    for t in range(count):
        row = rows[t]
        cols = [over_lanes(row, 8 * t + j) for j in range(8)]
        for k in range(8):
            pivot = 1.0 / over_rows(cols[k], k)
            here = sub == k
            row = jnp.where(lane == 8 * t + k, jnp.where(here, 1.0, 0.0), row)
            scaled = over_rows(row, k) * pivot
            row = jnp.where(here, scaled, row - cols[k] * scaled)
            for j in range(k + 1, 8):
                entry = over_rows(cols[j], k) * pivot
                cols[j] = jnp.where(here, entry, cols[j] - cols[k] * entry)
        rows[t] = row
        spread = [over_rows(row, j) for j in range(8)]
        inside = (lane >= 8 * t) & (lane < 8 * t + 8)
        for i in range(count):
            if i != t:
                terms = [over_lanes(rows[i], 8 * t + j) * spread[j] for j in range(8)]
                rows[i] = jnp.where(inside, 0.0, rows[i]) - tree(terms)
    for at in range(count):
        ref[which, 8 * at : 8 * at + 8, :] = rows[at]


def invert_first(m_ref, half_ref, cross_ref):
    h = m_ref.shape[0] // 2
    half_ref[0] = m_ref[:h, :h]
    invert_half(half_ref, 0)
    cross = mul(half_ref[0], m_ref[:h, h:])
    cross_ref[...] = cross
    half_ref[1] = m_ref[h:, h:] - mul(m_ref[h:, :h], cross)


def invert_last(half_ref, cross_ref, out_ref):
    h = cross_ref.shape[0]
    invert_half(half_ref, 1)
    cross, last = cross_ref[...], half_ref[1]
    corner = mul(cross, last)
    out_ref[:h, :h] = half_ref[0] + mul(corner, cross, NT)
    out_ref[:h, h:] = -corner
    out_ref[h:, :h] = -mul(last, cross, NT)
    out_ref[h:, h:] = last


def invert_scratch(rank):
    h = rank // 2
    return [pltpu.VMEM((rank, rank), F32), pltpu.VMEM((2, h, h), F32), pltpu.VMEM((h, h), F32)]


def on_device(n_ia, n_ja, n_ka, tensor, factor_b, factor_c):
    i_dev, j_dev, k_dev = tensor.shape
    rank = factor_b.shape[-1]
    n_a, n_b, n_c = n_ja * n_ka, n_ia * n_ka, n_ia * n_ja
    a_rows, b_rows, c_rows = i_dev // n_a, j_dev // n_b, k_dev // n_c
    h = rank // 2
    packed = h + h // 2
    ia_bits, ja_bits, ka_bits = bits("ia", n_ia), bits("ja", n_ja), bits("ka", n_ka)
    place = jnp.stack([lax.axis_index(axis) for axis in ("ia", "ja", "ka")]).astype(jnp.int32)
    vmem = pl.BlockSpec(memory_space=pltpu.VMEM)
    smem = pl.BlockSpec(memory_space=pltpu.SMEM)
    i_step = 16
    steps = i_dev // i_step
    depth = i_step * j_dev
    size = i_dev * j_dev * k_dev

    def span(s, length):
        return pl.ds(pl.multiple_of(s * length, length), length)

    def call(kernel, name, ins, outs, grid=(), in_specs=None, out_specs=None, scratch=(), flops=0, moved=1 << 20):
        in_specs = in_specs or [vmem] * len(ins)
        out_specs = out_specs or [vmem] * len(outs)
        return pl.pallas_call(
            kernel,
            grid=grid,
            out_shape=[jax.ShapeDtypeStruct(shape, dtype) for shape, dtype in outs],
            in_specs=in_specs,
            out_specs=out_specs,
            scratch_shapes=list(scratch),
            compiler_params=pltpu.CompilerParams(vmem_limit_bytes=VMEM_LIMIT),
            cost_estimate=pl.CostEstimate(flops=flops, bytes_accessed=moved, transcendentals=0),
            name=name,
        )(*ins)

    def pack_kernel(c_ref, b_ref, out_ref, c_buffer, b_buffer, sems):
        copies = [
            pltpu.make_async_copy(c_ref, c_buffer, sems.at[0]),
            pltpu.make_async_copy(b_ref, b_buffer, sems.at[1]),
        ]
        for copy in copies:
            copy.start()
        for copy in copies:
            copy.wait()
        out_ref[:c_rows, :] = c_buffer[0]
        out_ref[c_rows:, :] = b_buffer[0]

    hbm = pl.BlockSpec(memory_space=pltpu.HBM)
    (given,) = call(
        pack_kernel,
        "pack",
        [pltpu.with_memory_space_constraint(factor, pltpu.HBM) for factor in (factor_c, factor_b)],
        [((c_rows + b_rows, rank), F32)],
        in_specs=[hbm, hbm],
        scratch=[pltpu.VMEM(factor_c.shape, F32), pltpu.VMEM(factor_b.shape, F32), pltpu.SemaphoreType.DMA((2,))],
    )
    others = [swap(given, "ia", q) for q in range(1, n_ia)]

    def load_kernel(t_ref, high_ref, low_ref, buffer_ref, sems):
        copies = [
            pltpu.make_async_copy(
                t_ref.at[pl.ds(s * i_step, i_step)], buffer_ref.at[pl.ds(s * i_step, i_step)], sems.at[s]
            )
            for s in range(steps)
        ]
        for copy in copies:
            copy.start()
        for s, copy in enumerate(copies):
            copy.wait()
            high, low = split(buffer_ref[s * i_step : (s + 1) * i_step].reshape(depth, k_dev))
            high_ref[s * depth : (s + 1) * depth, :] = high
            low_ref[s * depth : (s + 1) * depth, :] = low

    t_parts = call(
        load_kernel,
        "load",
        [pltpu.with_memory_space_constraint(tensor, pltpu.HBM)],
        [((i_dev * j_dev, k_dev), BF16)] * 2,
        in_specs=[hbm],
        scratch=[pltpu.VMEM((i_dev, j_dev, k_dev), F32), pltpu.SemaphoreType.DMA((steps,))],
        moved=8 * size,
    )
    *others, t_high, t_low = lax.optimization_barrier((*others, *t_parts))
    both = jnp.stack([given, *others])
    c_blocks = grow(both[:, :c_rows].reshape(n_ia * c_rows, rank), ja_bits)
    b_blocks = grow(both[:, c_rows:].reshape(n_ia * b_rows, rank), ka_bits)

    def given_kernel(place_ref, c_ref, b_ref, gram_ref, tall_ref, b_out, whole_c, whole_b):
        left, right = c_ref[:, :h], c_ref[:, h:]
        gram_ref[:h, :] = mul(left, left, TN)
        gram_ref[h : 2 * h, :] = mul(left, right, TN)
        gram_ref[2 * h :, :] = mul(right, right, TN)
        ia, ja, ka = place_ref[0], place_ref[1], place_ref[2]
        for p in range(n_c):
            masks = origin(p, ia_bits[::-1] + ja_bits)
            whole_c[(ia ^ masks["ia"]) * n_ja + (ja ^ masks["ja"])] = c_ref[p * c_rows : (p + 1) * c_rows, :]
        for p in range(n_b):
            masks = origin(p, ia_bits[::-1] + ka_bits)
            whole_b[(ia ^ masks["ia"]) * n_ka + (ka ^ masks["ka"])] = b_ref[p * b_rows : (p + 1) * b_rows, :]
        b_out[...] = whole_b[...].reshape(j_dev, rank)
        high, low = split(whole_c[...].reshape(k_dev, rank))
        tall_ref[:k_dev, :] = high
        tall_ref[k_dev : 2 * k_dev, :] = high
        tall_ref[2 * k_dev :, :] = low

    gram_c_part, tall, b_slice = call(
        given_kernel,
        "given",
        [place, c_blocks, b_blocks],
        [((3 * h, h), F32), ((3 * k_dev, rank), BF16), ((j_dev, rank), F32)],
        in_specs=[smem, vmem, vmem],
        scratch=[pltpu.VMEM((n_c, c_rows, rank), F32), pltpu.VMEM((n_b, b_rows, rank), F32)],
        flops=2 * 6 * k_dev * rank * rank,
    )
    gram_c = gram_c_part
    for axis, distance in ka_bits:
        gram_c = gram_c + swap(gram_c, axis, distance)
    all_b = grow(b_blocks, ja_bits[::-1])

    def first_kernel(high_ref, low_ref, tall_ref, b_ref, y_ref, out_ref):
        def step(s, _):
            high, low = high_ref[span(s, depth), :], low_ref[span(s, depth), :]
            wide = jnp.concatenate([high, low, high], axis=1)
            inner = lax.dot_general(wide, tall_ref[...], NN, preferred_element_type=F32).reshape(i_step, j_dev, rank)
            y_ref[span(s, i_step)] = inner
            out_ref[span(s, i_step), :] = jnp.sum(inner * b_ref[...].reshape(1, j_dev, rank), axis=1)
            return 0

        lax.fori_loop(0, steps, step, 0)

    y, parts_a = call(
        first_kernel,
        "first",
        [t_high, t_low, tall, b_slice],
        [((i_dev, j_dev, rank), F32), ((i_dev, rank), F32)],
        flops=6 * size * rank,
        moved=8 * size,
    )

    def invert_a_first_kernel(packed_ref, b_ref, half_ref, cross_ref, gram_ref, m_ref):
        gram_ref[:h, :h] = packed_ref[:h, :]
        gram_ref[:h, h:] = packed_ref[h : 2 * h, :]
        gram_ref[h:, :h] = packed_ref[h : 2 * h, :].T
        gram_ref[h:, h:] = packed_ref[2 * h :, :]
        b = b_ref[...]
        m_ref[...] = gram_ref[...] * mul(b, b, TN)
        invert_first(m_ref, half_ref, cross_ref)

    halves, cross, gram_c = call(
        invert_a_first_kernel,
        "invert_a_first",
        [gram_c, all_b],
        [((2, h, h), F32), ((h, h), F32), ((rank, rank), F32)],
        scratch=[pltpu.VMEM((rank, rank), F32)],
        flops=5 * 1000 * 1000 * 1000,
    )

    def invert_last_kernel(half_in, cross_ref, out_ref, half_ref):
        half_ref[...] = half_in[...]
        invert_last(half_ref, cross_ref, out_ref)

    stages = [pair for pair in ja_bits if pair[1] > 1] + ka_bits + [pair for pair in ja_bits if pair[1] == 1]
    for at, (axis, distance) in enumerate(stages[:-1]):
        other_a = swap(parts_a, axis, distance)
        if at == 0:
            halves, cross, other_a = lax.optimization_barrier((halves, cross, other_a))
            (inverse_a,) = call(
                invert_last_kernel,
                "invert_a_last",
                [halves, cross],
                [((rank, rank), F32)],
                scratch=[pltpu.VMEM((2, h, h), F32)],
                flops=5 * 1000 * 1000 * 1000,
            )
        if at == 1:
            inverse_a, other_a = lax.optimization_barrier((inverse_a, other_a))
        parts_a = parts_a + other_a
    other_a = swap(parts_a, *stages[-1])

    def solve_a_kernel(place_ref, one_ref, other_ref, inverse_ref, a_ref, own_ref, gram_ref, rows_ref, packed_ref):
        a = mul(one_ref[...] + other_ref[...], inverse_ref[...])
        a_ref[...] = a
        rows_ref[...] = a.reshape(n_a, a_rows, rank)
        own_ref[...] = rows_ref[place_ref[1] * n_ka + place_ref[2]]
        left, right = a[:, :h], a[:, h:]
        middle = mul(left, right, TN)
        packed_ref[0, :h, :] = mul(left, left, TN)
        packed_ref[0, h:, :] = middle[: h // 2]
        packed_ref[1, :h, :] = mul(right, right, TN)
        packed_ref[1, h:, :] = middle[h // 2 :]
        gram_ref[...] = packed_ref[place_ref[1] & 1]

    a_slice, new_a, gram_a = call(
        solve_a_kernel,
        "solve_a",
        [place, parts_a, other_a, inverse_a],
        [((i_dev, rank), F32), ((a_rows, rank), F32), ((packed, h), F32)],
        in_specs=[smem, vmem, vmem, vmem],
        scratch=[pltpu.VMEM((n_a, a_rows, rank), F32), pltpu.VMEM((2, packed, h), F32)],
    )
    far_gram = swap(gram_a, *ia_bits[0])

    def second_kernel(y_ref, a_ref, out_ref):
        def step(s, total):
            return total + jnp.sum(y_ref[span(s, i_step)] * a_ref[span(s, i_step), :][:, None, :], axis=0)

        out_ref[...] = lax.fori_loop(0, steps, step, jnp.zeros((j_dev, rank), F32))

    (parts_b,) = call(
        second_kernel,
        "second",
        [y, a_slice],
        [((j_dev, rank), F32)],
        flops=2 * i_dev * j_dev * rank,
        moved=4 * i_dev * j_dev * rank,
    )
    t_high, t_low, parts_b = lax.optimization_barrier((t_high, t_low, parts_b))

    def turn_kernel(high_ref, low_ref, out_ref):
        def step(s, _):
            out_ref[:k_dev, span(s, depth)] = high_ref[span(s, depth), :].T
            out_ref[k_dev:, span(s, depth)] = low_ref[span(s, depth), :].T
            return 0

        lax.fori_loop(0, steps, step, 0)

    (turned,) = call(
        turn_kernel, "turn", [t_high, t_low], [((2 * k_dev, i_dev * j_dev), BF16)], moved=8 * size
    )
    stages_b = ka_bits + ia_bits
    other_b = swap(parts_b, *stages_b[0])
    far_gram, turned, other_b = lax.optimization_barrier((far_gram, turned, other_b))
    gram_a = gram_a + far_gram
    parts_b = parts_b + other_b
    for axis, distance in ia_bits[1:]:
        near_gram = swap(gram_a, axis, distance)
        gram_a = gram_a + near_gram
    gram_a_other = swap(gram_a, "ja", 1)

    def invert_b_first_kernel(place_ref, one_ref, other_ref, gram_c_ref, gram_ref, half_ref, cross_ref, packed_ref, m_ref):
        core = place_ref[1] & 1
        packed_ref[core] = one_ref[...]
        packed_ref[core ^ 1] = other_ref[...]
        gram_ref[:h, :h] = packed_ref[0, :h, :]
        gram_ref[h:, h:] = packed_ref[1, :h, :]
        gram_ref[: h // 2, h:] = packed_ref[0, h:, :]
        gram_ref[h // 2 : h, h:] = packed_ref[1, h:, :]
        gram_ref[h:, :h] = gram_ref[:h, h:].T
        m_ref[...] = gram_ref[...] * gram_c_ref[...]
        invert_first(m_ref, half_ref, cross_ref)

    gram_a, halves, cross = call(
        invert_b_first_kernel,
        "invert_b_first",
        [place, gram_a, gram_a_other, gram_c],
        [((rank, rank), F32), ((2, h, h), F32), ((h, h), F32)],
        in_specs=[smem, vmem, vmem, vmem],
        scratch=[pltpu.VMEM((2, packed, h), F32), pltpu.VMEM((rank, rank), F32)],
        flops=5 * 1000 * 1000 * 1000,
    )

    for at, (axis, distance) in enumerate(stages_b[1:-1], 1):
        other_b = swap(parts_b, axis, distance)
        if at == len(stages_b) - 2:
            halves, cross, other_b = lax.optimization_barrier((halves, cross, other_b))
        parts_b = parts_b + other_b
    other_b = swap(parts_b, *stages_b[-1])
    (inverse_b,) = call(
        invert_last_kernel,
        "invert_b_last",
        [halves, cross],
        [((rank, rank), F32)],
        scratch=[pltpu.VMEM((2, h, h), F32)],
        flops=5 * 1000 * 1000 * 1000,
    )

    def solve_b_kernel(place_ref, one_ref, other_ref, inverse_ref, b_ref, own_ref, rows_ref):
        b = mul(one_ref[...] + other_ref[...], inverse_ref[...])
        b_ref[...] = b
        rows_ref[...] = b.reshape(n_b, b_rows, rank)
        own_ref[...] = rows_ref[place_ref[0] * n_ka + place_ref[2]]

    b_new_slice, new_b = call(
        solve_b_kernel,
        "solve_b",
        [place, parts_b, other_b, inverse_b],
        [((j_dev, rank), F32), ((b_rows, rank), F32)],
        in_specs=[smem, vmem, vmem, vmem],
        scratch=[pltpu.VMEM((n_b, b_rows, rank), F32)],
    )

    first_b = swap(b_new_slice, *ja_bits[0])

    def third_kernel(turned_ref, a_ref, b_ref, out_ref):
        def step(s, total):
            high, low = split((a_ref[span(s, i_step), :][:, None, :] * b_ref[...][None]).reshape(depth, rank))
            both = lax.dot_general(turned_ref[:, span(s, depth)], high, NN, preferred_element_type=F32)
            more = lax.dot_general(turned_ref[:k_dev, span(s, depth)], low, NN, preferred_element_type=F32)
            return total + (both[:k_dev] + (both[k_dev:] + more))

        out_ref[...] = lax.fori_loop(0, steps, step, jnp.zeros((k_dev, rank), F32))

    (parts_c,) = call(
        third_kernel,
        "third",
        [turned, a_slice, b_new_slice],
        [((k_dev, rank), F32)],
        flops=6 * size * rank,
        moved=4 * size,
    )
    first_b, parts_c = lax.optimization_barrier((first_b, parts_c))
    all_b_new = grow(jnp.concatenate([b_new_slice, first_b], axis=0), ja_bits[1:])
    sums_c = lax.all_to_all(parts_c.reshape(n_c, c_rows, rank), ("ia", "ja"), split_axis=0, concat_axis=0)

    def invert_c_kernel(b_ref, gram_a_ref, inverse_ref, m_ref, half_ref, cross_ref):
        b = b_ref[...]
        m_ref[...] = gram_a_ref[...] * mul(b, b, TN)
        invert_first(m_ref, half_ref, cross_ref)
        invert_last(half_ref, cross_ref, inverse_ref)

    (inverse_c,) = call(
        invert_c_kernel,
        "invert_c",
        [all_b_new, gram_a],
        [((rank, rank), F32)],
        scratch=invert_scratch(rank),
        flops=10 * 1000 * 1000 * 1000,
    )

    def solve_c_kernel(sums_ref, inverse_ref, out_ref):
        out_ref[...] = mul(tree(sums_ref[q] for q in range(n_c)), inverse_ref[...])

    (new_c,) = call(solve_c_kernel, "solve_c", [sums_c, inverse_c], [((c_rows, rank), F32)])
    return (new_a[None], new_b[None], new_c[None])


def solution(mesh):
    sizes = [mesh.shape[axis] for axis in ("ia", "ja", "ka")]
    return jax.shard_map(
        functools.partial(on_device, *sizes),
        mesh=mesh,
        in_specs=(P("ia", "ja", "ka"), P("ja", ("ia", "ka"), None), P("ka", ("ia", "ja"), None)),
        out_specs=(
            P("ia", ("ja", "ka"), None),
            P("ja", ("ia", "ka"), None),
            P("ka", ("ia", "ja"), None),
        ),
        check_vma=False,
    )
```

time: 730 us -> 90 us (0.12)
  waiting for transfers between devices: 334 us -> 9.38 us
  other arithmetic: 168 us -> 0.3 us
  blocking collectives: 98.9 us -> 0 us
  matrix products: 86 us -> 0 us
  Pallas kernels: 0 us -> 52.5 us
  starting transfers between devices: 0.83 us -> 26.5 us
  between operations: 19.8 us -> 0.89 us
  local copies, waits for them, and re-layouts: 16.5 us -> 0.01 us
    psum x3 -> x0, waiting for transfers between devices: 303 us -> none  [the longest x1 108 us: on_device(): gram_b_new = lax.psum(gram_of(new_b), ('ia', 'ja', 'ka'))]
    another operation x27 -> x2, other arithmetic: 162 us -> 0.09 us  [the longest x1 0.08 us: on_device(): jnp.stack([lax.axis_index(axis) for axis in ('ia', 'ja', 'ka')])]
    all_gather x4 -> x0, blocking collectives: 98.9 us -> none  [the longest x1 32.5 us: on_device(): b_slice = lax.all_gather(factor_b, ('ia', 'ka'), axis=1, tiled=True)[0]]
    dot_general x8 -> x0, matrix products: 80.6 us -> none  [the longest x1 27.7 us: on_device(): partial_b = jnp.einsum('jkr,kr->jr', inner, c_slice, precision=HIGH)]
    pallas_call x0 -> x15, Pallas kernels: none -> 52.5 us  [call(): pl.pallas_call(kernel, grid=grid, out_shape=[jax.ShapeDtypeStruct(shape,...]
    unnamed x9 -> x0, waiting for transfers between devices: 31 us -> none
    ppermute x0 -> x20, starting transfers between devices: none -> 22.7 us  [swap(): lax.ppermute(value, axis, [(rank, rank ^ distance) for rank in range(lax....]
    another operation x28 -> x0, local copies, waits for them, and re-layouts: 11.9 us -> none  [the longest x16 7.89 us: solve_rows(): return jax.scipy.linalg.cho_solve((factor, True), right.T).T]
  transfers between devices with their start and end apart: 6 -> 21, of which waited for: 4 -> 9; matrix products, arithmetic and copies ran while one was open for 23% -> 0% of each run, Pallas kernels for 0% -> 54%
where the time goes in v1:
time: 90 us; the launch traced here: 89.6 us
  Pallas kernels  52.5 us (58%)
  starting transfers between devices  26.5 us (29%)
  waiting for transfers between devices  9.38 us (10%)
    pallas_call x15, Pallas kernels, call(): pl.pallas_call(kernel, grid=grid, out_shape=[jax.ShapeDtypeStruct(shape,...  52.5 us
    ppermute x20, starting transfers between devices, swap(): lax.ppermute(value, axis, [(rank, rank ^ distance) for rank in range(lax....  22.7 us
    ppermute x20, waiting for transfers between devices, swap(): lax.ppermute(value, axis, [(rank, rank ^ distance) for rank in range(lax....  9.23 us
    all_to_all x1, starting transfers between devices, on_device(): lax.all_to_all(parts_c.reshape(n_c, c_rows, rank), ('ia', 'ja'), split_ax...  3.8 us
  transfers between devices with their start and end apart: 21, of which 9 were waited for; matrix products, arithmetic and copies ran while one was open for 0% of the time, Pallas kernels for 54%

profile of v1, /device:TPU:0, one launch (start us, length us, event | category | flops | bytes accessed | tf_op | source)
XLA Modules:
  0.0 89.6 jit_solution(1577430793194645894)
XLA Ops:
  1.4 5.1 %collective-permute-start.2 = (f32[24,256]{1,0:T(8,128)S(1)}, f32[24,256]{1,0:T(8,128)S(1)}, u32[]{:S(2)}, u32[]{:S(2)}) collective-permute-start(f32[24,256]{1,0:T(8,128)S(1)} %pack.1), channel_id=1, source_target_pairs={{0,24},{8,16},{16,8},{24,0},{1,25},{9,17},{17,9},{25,1},{2,26},{10... | collective-permute-start | bytes 73736 | tf_op jit(solution)/shard_map/ppermute | solution.py:41
  7.1 3.6 %load.1 = (bf16[8192,256]{1,0:T(8,128)(2,1)S(1)}, bf16[8192,256]{1,0:T(8,128)(2,1)S(1)}) custom-call(f32[128,64,256]{2,1,0:T(8,128)} %t_ref.1), custom_call_target="tpu_custom_call" | custom-call | bytes 16777216 | tf_op jit(solution)/shard_map/load/pallas_call | solution.py:140
  11.2 1.5 %collective-permute-start.5 = (f32[32,256]{1,0:T(8,128)S(1)}, f32[32,256]{1,0:T(8,128)S(1)}, u32[]{:S(2)}, u32[]{:S(2)}) collective-permute-start(f32[32,256]{1,0:T(8,128)S(1)} %maximum_bitcast_fusion), channel_id=1, source_target_pairs={{0,1},{1,0},{2,3},{3,2},{4,5},{5,4},{6,7},{7,6},{8,9},{9,8},{10,11... | collective-permute-start | bytes 98312 | tf_op jit(solution)/shard_map/ppermute | solution.py:41
  12.8 1.6 %collective-permute-start.3 = (f32[64,256]{1,0:T(8,128)S(1)}, f32[64,256]{1,0:T(8,128)S(1)}, u32[]{:S(2)}, u32[]{:S(2)}) collective-permute-start(f32[64,256]{1,0:T(8,128)S(1)} %bitcast.16), channel_id=1, source_target_pairs={{0,4},{2,6},{4,0},{6,2},{1,5},{3,7},{5,1},{7,3},{8,12},{10,14},{12... | collective-permute-start | bytes 196616 | tf_op jit(solution)/shard_map/ppermute | solution.py:41
  15.2 1.9 %collective-permute-done.3 = f32[64,256]{1,0:T(8,128)S(1)} collective-permute-done((f32[64,256]{1,0:T(8,128)S(1)}, f32[64,256]{1,0:T(8,128)S(1)}, u32[]{:S(2)}, u32[]{:S(2)}) %collective-permute-start.3) | collective-permute-done | bytes 65568 | tf_op jit(solution)/shard_map/ppermute | solution.py:41
  17.3 1.6 %collective-permute-start.8 = (f32[128,256]{1,0:T(8,128)S(1)}, f32[128,256]{1,0:T(8,128)S(1)}, u32[]{:S(2)}, u32[]{:S(2)}) collective-permute-start(f32[128,256]{1,0:T(8,128)S(1)} %pad_maximum_fusion.4), channel_id=1, source_target_pairs={{0,4},{2,6},{4,0},{6,2},{1,5},{3,7},{5,1},{7,3},{8,12},{10,14},{12... | collective-permute-start | bytes 393224 | tf_op jit(solution)/shard_map/ppermute | solution.py:41
  20.7 4.7 %first.1 = (f32[128,64,256]{2,1,0:T(8,128)S(1)}, f32[128,256]{1,0:T(8,128)S(1)}) custom-call(bf16[8192,256]{1,0:T(8,128)(2,1)S(1)} %get-tuple-element.65.high_ref, bf16[8192,256]{1,0:T(8,128)(2,1)S(1)} %get-tuple-element.66.low_ref, bf16[768,256]{1,0:T(8,128)(2,1)S(1)} %get-tuple-element.49.tall_ref, f32[64,256]{1,0:T(8,128)S(1)} %get-tuple-element.50.b_ref), custom_call_target="tpu_custom_call" | custom-call | flops 3221225472 | bytes 16777216 | tf_op jit(solution)/shard_map/first/pallas_call | solution.py:140
  27.1 4.9 %invert_a_first.1 = (f32[2,128,128]{2,1,0:T(8,128)S(1)}, f32[128,128]{1,0:T(8,128)S(1)}, f32[256,256]{1,0:T(8,128)S(1)}) custom-call(f32[384,128]{1,0:T(8,128)S(1)} %add.21.packed_ref, f32[256,256]{1,0:T(8,128)S(1)} %pad_maximum_fusion.1.b_ref), custom_call_target="tpu_custom_call" | custom-call | flops 5000000000 | bytes 1048576 | tf_op jit(solution)/shard_map/invert_a_first/pallas_call | solution.py:140
  33.1 4.7 %invert_a_last.1.inverse_ref = f32[256,256]{1,0:T(8,128)S(1)} custom-call(f32[2,128,128]{2,1,0:T(8,128)S(1)} %get-tuple-element.56.half_in, f32[128,128]{1,0:T(8,128)S(1)} %get-tuple-element.57.cross_ref), custom_call_target="tpu_custom_call" | custom-call | flops 5000000000 | bytes 1048576 | tf_op jit(solution)/shard_map/invert_a_last/pallas_call | solution.py:140
  37.9 1.3 %collective-permute-done.11.other_ref = f32[128,256]{1,0:T(8,128)S(1)} collective-permute-done((f32[128,256]{1,0:T(8,128)S(1)}, f32[128,256]{1,0:T(8,128)S(1)}, u32[]{:S(2)}, u32[]{:S(2)}) %collective-permute-start.11) | collective-permute-done | bytes 131104 | tf_op jit(solution)/shard_map/ppermute | solution.py:41
  39.3 1.5 %solve_a.1 = (f32[128,256]{1,0:T(8,128)S(1)}, f32[16,256]{1,0:T(8,128)}, f32[192,128]{1,0:T(8,128)S(1)}) custom-call(s32[3]{0:T(128)S(1)} %pad_add_fusion.place_ref, f32[128,256]{1,0:T(8,128)S(1)} %add.23.one_ref, f32[128,256]{1,0:T(8,128)S(1)} %collective-permute-done.11.other_ref, f32[256,256]{1,0:T(8,128)S(1)} %invert_a_last.1.inverse_ref), custom_call_target="tpu_custom_call" | custom-call | bytes 1048576 | tf_op jit(solution)/shard_map/solve_a/pallas_call | solution.py:140
  40.8 2.0 %collective-permute-start.12 = (f32[192,128]{1,0:T(8,128)S(1)}, f32[192,128]{1,0:T(8,128)S(1)}, u32[]{:S(2)}, u32[]{:S(2)}) collective-permute-start(f32[192,128]{1,0:T(8,128)S(1)} %get-tuple-element.64), channel_id=1, source_target_pairs={{0,16},{8,24},{16,0},{24,8},{1,17},{9,25},{17,1},{25,9},{2,18},{10... | collective-permute-start | bytes 294920 | tf_op jit(solution)/shard_map/ppermute | solution.py:41
  43.7 1.1 %collective-permute-start.13 = (f32[64,256]{1,0:T(8,128)S(1)}, f32[64,256]{1,0:T(8,128)S(1)}, u32[]{:S(2)}, u32[]{:S(2)}) collective-permute-start(f32[64,256]{1,0:T(8,128)S(1)} %second.1), channel_id=1, source_target_pairs={{0,1},{1,0},{2,3},{3,2},{4,5},{5,4},{6,7},{7,6},{8,9},{9,8},{10,11... | collective-permute-start | bytes 196616 | tf_op jit(solution)/shard_map/ppermute | solution.py:41
  44.8 3.0 %turn.1.turned_ref = bf16[512,8192]{1,0:T(8,128)(2,1)S(1)} custom-call(bf16[8192,256]{1,0:T(8,128)(2,1)S(1)} %get-tuple-element.65.high_ref, bf16[8192,256]{1,0:T(8,128)(2,1)S(1)} %get-tuple-element.66.low_ref), custom_call_target="tpu_custom_call" | custom-call | bytes 16777216 | tf_op jit(solution)/shard_map/turn/pallas_call | solution.py:140
  48.6 1.4 %collective-permute-start.14 = (f32[192,128]{1,0:T(8,128)S(1)}, f32[192,128]{1,0:T(8,128)S(1)}, u32[]{:S(2)}, u32[]{:S(2)}) collective-permute-start(f32[192,128]{1,0:T(8,128)S(1)} %add.25), channel_id=1, source_target_pairs={{0,8},{8,0},{16,24},{24,16},{1,9},{9,1},{17,25},{25,17},{2,10},{10... | collective-permute-start | bytes 294920 | tf_op jit(solution)/shard_map/ppermute | solution.py:41
  50.1 3.3 %collective-permute-done.14 = f32[192,128]{1,0:T(8,128)S(1)} collective-permute-done((f32[192,128]{1,0:T(8,128)S(1)}, f32[192,128]{1,0:T(8,128)S(1)}, u32[]{:S(2)}, u32[]{:S(2)}) %collective-permute-start.14) | collective-permute-done | bytes 98336 | tf_op jit(solution)/shard_map/ppermute | solution.py:41
  53.4 1.9 %collective-permute-start.16 = (f32[64,256]{1,0:T(8,128)S(1)}, f32[64,256]{1,0:T(8,128)S(1)}, u32[]{:S(2)}, u32[]{:S(2)}) collective-permute-start(f32[64,256]{1,0:T(8,128)S(1)} %add.24), channel_id=1, source_target_pairs={{0,16},{8,24},{16,0},{24,8},{1,17},{9,25},{17,1},{25,9},{2,18},{10... | collective-permute-start | bytes 196616 | tf_op jit(solution)/shard_map/ppermute | solution.py:41
  55.4 5.2 %invert_b_first.1 = (f32[256,256]{1,0:T(8,128)S(1)}, f32[2,128,128]{2,1,0:T(8,128)S(1)}, f32[128,128]{1,0:T(8,128)S(1)}) custom-call(s32[3]{0:T(128)S(1)} %pad_add_fusion.place_ref, f32[192,128]{1,0:T(8,128)S(1)} %add.26.one_ref, f32[192,128]{1,0:T(8,128)S(1)} %collective-permute-done.15.other_ref, f32[256,256]{1,0:T(8,128)S(1)} %get-tuple-element.69.gram_c_ref), custom_call_target="tpu_custom_call" | custom-call | flops 5000000000 | bytes 1048576 | tf_op jit(solution)/shard_map/invert_b_first/pallas_call | solution.py:140
  60.6 1.8 %collective-permute-start.17 = (f32[64,256]{1,0:T(8,128)S(1)}, f32[64,256]{1,0:T(8,128)S(1)}, u32[]{:S(2)}, u32[]{:S(2)}) collective-permute-start(f32[64,256]{1,0:T(8,128)S(1)} %add.27.one_ref), channel_id=1, source_target_pairs={{0,8},{8,0},{16,24},{24,16},{1,9},{9,1},{17,25},{25,17},{2,10},{10... | collective-permute-start | bytes 196616 | tf_op jit(solution)/shard_map/ppermute | solution.py:41
  62.4 4.7 %invert_b_last.1.inverse_ref = f32[256,256]{1,0:T(8,128)S(1)} custom-call(f32[2,128,128]{2,1,0:T(8,128)S(1)} %get-tuple-element.73.half_in, f32[128,128]{1,0:T(8,128)S(1)} %get-tuple-element.74.cross_ref), custom_call_target="tpu_custom_call" | custom-call | flops 5000000000 | bytes 1048576 | tf_op jit(solution)/shard_map/invert_b_last/pallas_call | solution.py:140
  67.2 1.4 %solve_b.1 = (f32[64,256]{1,0:T(8,128)S(1)}, f32[8,256]{1,0:T(8,128)}) custom-call(s32[3]{0:T(128)S(1)} %pad_add_fusion.place_ref, f32[64,256]{1,0:T(8,128)S(1)} %add.27.one_ref, f32[64,256]{1,0:T(8,128)S(1)} %collective-permute-done.17.other_ref, f32[256,256]{1,0:T(8,128)S(1)} %invert_b_last.1.inverse_ref), custom_call_target="tpu_custom_call" | custom-call | bytes 1048576 | tf_op jit(solution)/shard_map/solve_b/pallas_call | solution.py:140
  69.4 5.7 %third.1 = f32[256,256]{1,0:T(8,128)} custom-call(bf16[512,8192]{1,0:T(8,128)(2,1)S(1)} %turn.1.turned_ref, f32[128,256]{1,0:T(8,128)S(1)} %get-tuple-element.62.a_ref, f32[64,256]{1,0:T(8,128)S(1)} %get-tuple-element.76.b_ref), custom_call_target="tpu_custom_call" | custom-call | flops 3221225472 | bytes 8388608 | tf_op jit(solution)/shard_map/third/pallas_call | solution.py:140
  75.2 3.8 %all-to-all-start = ((f32[16,16,256]{2,1,0:T(8,128)}), f32[16,16,256]{2,1,0:T(8,128)S(1)}, u32[]{:S(2)}, u32[]{:S(2)}) async-start(f32[16,16,256]{2,1,0:T(8,128)} %bitcast.11), calls=%async_computation | async-start | bytes 524288 | tf_op jit(solution)/shard_map/all_to_all | solution.py:429
  79.0 9.6 %invert_c.1.inverse_ref = f32[256,256]{1,0:T(8,128)S(1)} custom-call(f32[256,256]{1,0:T(8,128)S(1)} %pad_maximum_fusion.2.b_ref, f32[256,256]{1,0:T(8,128)S(1)} %get-tuple-element.80.gram_a_ref), custom_call_target="tpu_custom_call" | custom-call | flops 10000000000 | bytes 1048576 | tf_op jit(solution)/shard_map/invert_c/pallas_call | solution.py:140
  (51 shorter events, 11.4 us)
Async XLA Ops:
  1.4 9.4 %collective-permute-start.2 = (f32[24,256]{1,0:T(8,128)S(1)}, f32[24,256]{1,0:T(8,128)S(1)}, u32[]{:S(2)}, u32[]{:S(2)}) collective-permute-start(f32[24,256]{1,0:T(8,128)S(1)} %pack.1), channel_id=1, source_target_pairs={{0,24},{8,16},{16,8},{24,0},{1,25},{9,17},{17,9},{25,1},{2,26},{10... | collective-permute-start | bytes 73736 | tf_op jit(solution)/shard_map/ppermute | solution.py:41
  6.5 4.7 %collective-permute-start.1 = (f32[24,256]{1,0:T(8,128)S(1)}, f32[24,256]{1,0:T(8,128)S(1)}, u32[]{:S(2)}, u32[]{:S(2)}) collective-permute-start(f32[24,256]{1,0:T(8,128)S(1)} %pack.1), channel_id=1, source_target_pairs={{0,16},{8,24},{16,0},{24,8},{1,17},{9,25},{17,1},{25,9},{2,18},{10... | collective-permute-start | bytes 73736 | tf_op jit(solution)/shard_map/ppermute | solution.py:41
  6.5 4.7 %collective-permute-start = (f32[24,256]{1,0:T(8,128)S(1)}, f32[24,256]{1,0:T(8,128)S(1)}, u32[]{:S(2)}, u32[]{:S(2)}) collective-permute-start(f32[24,256]{1,0:T(8,128)S(1)} %pack.1), channel_id=1, source_target_pairs={{0,8},{8,0},{16,24},{24,16},{1,9},{9,1},{17,25},{25,17},{2,10},{10... | collective-permute-start | bytes 73736 | tf_op jit(solution)/shard_map/ppermute | solution.py:41
  11.2 3.9 %collective-permute-start.5 = (f32[32,256]{1,0:T(8,128)S(1)}, f32[32,256]{1,0:T(8,128)S(1)}, u32[]{:S(2)}, u32[]{:S(2)}) collective-permute-start(f32[32,256]{1,0:T(8,128)S(1)} %maximum_bitcast_fusion), channel_id=1, source_target_pairs={{0,1},{1,0},{2,3},{3,2},{4,5},{5,4},{6,7},{7,6},{8,9},{9,8},{10,11... | collective-permute-start | bytes 98312 | tf_op jit(solution)/shard_map/ppermute | solution.py:41
  12.8 4.3 %collective-permute-start.3 = (f32[64,256]{1,0:T(8,128)S(1)}, f32[64,256]{1,0:T(8,128)S(1)}, u32[]{:S(2)}, u32[]{:S(2)}) collective-permute-start(f32[64,256]{1,0:T(8,128)S(1)} %bitcast.16), channel_id=1, source_target_pairs={{0,4},{2,6},{4,0},{6,2},{1,5},{3,7},{5,1},{7,3},{8,12},{10,14},{12... | collective-permute-start | bytes 196616 | tf_op jit(solution)/shard_map/ppermute | solution.py:41
  15.1 2.1 %collective-permute-start.7 = (f32[64,256]{1,0:T(8,128)S(1)}, f32[64,256]{1,0:T(8,128)S(1)}, u32[]{:S(2)}, u32[]{:S(2)}) collective-permute-start(f32[64,256]{1,0:T(8,128)S(1)} %pad_maximum_fusion.7.b_ref), channel_id=1, source_target_pairs={{0,2},{2,0},{4,6},{6,4},{1,3},{3,1},{5,7},{7,5},{8,10},{10,8},{12,... | collective-permute-start | bytes 196616 | tf_op jit(solution)/shard_map/ppermute | solution.py:41
  17.1 1.7 %collective-permute-start.4 = (f32[128,256]{1,0:T(8,128)S(1)}, f32[128,256]{1,0:T(8,128)S(1)}, u32[]{:S(2)}, u32[]{:S(2)}) collective-permute-start(f32[128,256]{1,0:T(8,128)S(1)} %pad_maximum_fusion.3), channel_id=1, source_target_pairs={{0,2},{2,0},{4,6},{6,4},{1,3},{3,1},{5,7},{7,5},{8,10},{10,8},{12,... | collective-permute-start | bytes 393224 | tf_op jit(solution)/shard_map/ppermute | solution.py:41
  17.3 9.2 %collective-permute-start.8 = (f32[128,256]{1,0:T(8,128)S(1)}, f32[128,256]{1,0:T(8,128)S(1)}, u32[]{:S(2)}, u32[]{:S(2)}) collective-permute-start(f32[128,256]{1,0:T(8,128)S(1)} %pad_maximum_fusion.4), channel_id=1, source_target_pairs={{0,4},{2,6},{4,0},{6,2},{1,5},{3,7},{5,1},{7,3},{8,12},{10,14},{12... | collective-permute-start | bytes 393224 | tf_op jit(solution)/shard_map/ppermute | solution.py:41
  19.9 7.1 %collective-permute-start.6 = (f32[384,128]{1,0:T(8,128)S(1)}, f32[384,128]{1,0:T(8,128)S(1)}, u32[]{:S(2)}, u32[]{:S(2)}) collective-permute-start(f32[384,128]{1,0:T(8,128)S(1)} %get-tuple-element.52), channel_id=1, source_target_pairs={{0,1},{1,0},{2,3},{3,2},{4,5},{5,4},{6,7},{7,6},{8,9},{9,8},{10,11... | collective-permute-start | bytes 589832 | tf_op jit(solution)/shard_map/ppermute | solution.py:41
  25.4 6.6 %collective-permute-start.9 = (f32[128,256]{1,0:T(8,128)S(1)}, f32[128,256]{1,0:T(8,128)S(1)}, u32[]{:S(2)}, u32[]{:S(2)}) collective-permute-start(f32[128,256]{1,0:T(8,128)S(1)} %get-tuple-element.51), channel_id=1, source_target_pairs={{0,4},{2,6},{4,0},{6,2},{1,5},{3,7},{5,1},{7,3},{8,12},{10,14},{12... | collective-permute-start | bytes 393224 | tf_op jit(solution)/shard_map/ppermute | solution.py:41
  32.0 5.8 %collective-permute-start.10 = (f32[128,256]{1,0:T(8,128)S(1)}, f32[128,256]{1,0:T(8,128)S(1)}, u32[]{:S(2)}, u32[]{:S(2)}) collective-permute-start(f32[128,256]{1,0:T(8,128)S(1)} %add.22), channel_id=1, source_target_pairs={{0,1},{1,0},{2,3},{3,2},{4,5},{5,4},{6,7},{7,6},{8,9},{9,8},{10,11... | collective-permute-start | bytes 393224 | tf_op jit(solution)/shard_map/ppermute | solution.py:41
  37.8 1.4 %collective-permute-start.11 = (f32[128,256]{1,0:T(8,128)S(1)}, f32[128,256]{1,0:T(8,128)S(1)}, u32[]{:S(2)}, u32[]{:S(2)}) collective-permute-start(f32[128,256]{1,0:T(8,128)S(1)} %add.23.one_ref), channel_id=1, source_target_pairs={{0,2},{2,0},{4,6},{6,4},{1,3},{3,1},{5,7},{7,5},{8,10},{10,8},{12,... | collective-permute-start | bytes 393224 | tf_op jit(solution)/shard_map/ppermute | solution.py:41
  40.8 7.9 %collective-permute-start.12 = (f32[192,128]{1,0:T(8,128)S(1)}, f32[192,128]{1,0:T(8,128)S(1)}, u32[]{:S(2)}, u32[]{:S(2)}) collective-permute-start(f32[192,128]{1,0:T(8,128)S(1)} %get-tuple-element.64), channel_id=1, source_target_pairs={{0,16},{8,24},{16,0},{24,8},{1,17},{9,25},{17,1},{25,9},{2,18},{10... | collective-permute-start | bytes 294920 | tf_op jit(solution)/shard_map/ppermute | solution.py:41
  43.7 4.3 %collective-permute-start.13 = (f32[64,256]{1,0:T(8,128)S(1)}, f32[64,256]{1,0:T(8,128)S(1)}, u32[]{:S(2)}, u32[]{:S(2)}) collective-permute-start(f32[64,256]{1,0:T(8,128)S(1)} %second.1), channel_id=1, source_target_pairs={{0,1},{1,0},{2,3},{3,2},{4,5},{5,4},{6,7},{7,6},{8,9},{9,8},{10,11... | collective-permute-start | bytes 196616 | tf_op jit(solution)/shard_map/ppermute | solution.py:41
  48.6 4.7 %collective-permute-start.14 = (f32[192,128]{1,0:T(8,128)S(1)}, f32[192,128]{1,0:T(8,128)S(1)}, u32[]{:S(2)}, u32[]{:S(2)}) collective-permute-start(f32[192,128]{1,0:T(8,128)S(1)} %add.25), channel_id=1, source_target_pairs={{0,8},{8,0},{16,24},{24,16},{1,9},{9,1},{17,25},{25,17},{2,10},{10... | collective-permute-start | bytes 294920 | tf_op jit(solution)/shard_map/ppermute | solution.py:41
  53.3 2.0 %collective-permute-start.15 = (f32[192,128]{1,0:T(8,128)S(1)}, f32[192,128]{1,0:T(8,128)S(1)}, u32[]{:S(2)}, u32[]{:S(2)}) collective-permute-start(f32[192,128]{1,0:T(8,128)S(1)} %add.26.one_ref), channel_id=1, source_target_pairs={{0,2},{2,0},{4,6},{6,4},{1,3},{3,1},{5,7},{7,5},{8,10},{10,8},{12,... | collective-permute-start | bytes 294920 | tf_op jit(solution)/shard_map/ppermute | solution.py:41
  53.4 7.1 %collective-permute-start.16 = (f32[64,256]{1,0:T(8,128)S(1)}, f32[64,256]{1,0:T(8,128)S(1)}, u32[]{:S(2)}, u32[]{:S(2)}) collective-permute-start(f32[64,256]{1,0:T(8,128)S(1)} %add.24), channel_id=1, source_target_pairs={{0,16},{8,24},{16,0},{24,8},{1,17},{9,25},{17,1},{25,9},{2,18},{10... | collective-permute-start | bytes 196616 | tf_op jit(solution)/shard_map/ppermute | solution.py:41
  60.6 6.5 %collective-permute-start.17 = (f32[64,256]{1,0:T(8,128)S(1)}, f32[64,256]{1,0:T(8,128)S(1)}, u32[]{:S(2)}, u32[]{:S(2)}) collective-permute-start(f32[64,256]{1,0:T(8,128)S(1)} %add.27.one_ref), channel_id=1, source_target_pairs={{0,8},{8,0},{16,24},{24,16},{1,9},{9,1},{17,25},{25,17},{2,10},{10... | collective-permute-start | bytes 196616 | tf_op jit(solution)/shard_map/ppermute | solution.py:41
  68.5 6.5 %collective-permute-start.18 = (f32[64,256]{1,0:T(8,128)S(1)}, f32[64,256]{1,0:T(8,128)S(1)}, u32[]{:S(2)}, u32[]{:S(2)}) collective-permute-start(f32[64,256]{1,0:T(8,128)S(1)} %get-tuple-element.76.b_ref), channel_id=1, source_target_pairs={{0,4},{2,6},{4,0},{6,2},{1,5},{3,7},{5,1},{7,3},{8,12},{10,14},{12... | collective-permute-start | bytes 196616 | tf_op jit(solution)/shard_map/ppermute | solution.py:41
  75.1 3.9 %collective-permute-start.19 = (f32[128,256]{1,0:T(8,128)S(1)}, f32[128,256]{1,0:T(8,128)S(1)}, u32[]{:S(2)}, u32[]{:S(2)}) collective-permute-start(f32[128,256]{1,0:T(8,128)S(1)} %pad_maximum_fusion.5), channel_id=1, source_target_pairs={{0,2},{2,0},{4,6},{6,4},{1,3},{3,1},{5,7},{7,5},{8,10},{10,8},{12,... | collective-permute-start | bytes 393224 | tf_op jit(solution)/shard_map/ppermute | solution.py:41
  75.2 13.6 %all-to-all-start = ((f32[16,16,256]{2,1,0:T(8,128)}), f32[16,16,256]{2,1,0:T(8,128)S(1)}, u32[]{:S(2)}, u32[]{:S(2)}) async-start(f32[16,16,256]{2,1,0:T(8,128)} %bitcast.11), calls=%async_computation | async-start | bytes 524288 | tf_op jit(solution)/shard_map/all_to_all | solution.py:429

commit v2 on v1

--- a/solution.py
+++ b/solution.py
@@ -23,6 +23,13 @@
 def split(value):
     high = value.astype(BF16)
     return high, (value - high.astype(F32)).astype(BF16)
+
+
+def mul3(left, right, dims=NN):
+    (left_high, left_low), (right_high, right_low) = split(left), split(right)
+    left = jnp.concatenate([left_high, left_low, left_high], axis=dims[0][0][0])
+    right = jnp.concatenate([right_high, right_high, right_low], axis=dims[0][1][0])
+    return lax.dot_general(left, right, dims, preferred_element_type=F32)
 
 
 def tree(values):
@@ -203,9 +210,9 @@
 
     def given_kernel(place_ref, c_ref, b_ref, gram_ref, tall_ref, b_out, whole_c, whole_b):
         left, right = c_ref[:, :h], c_ref[:, h:]
-        gram_ref[:h, :] = mul(left, left, TN)
-        gram_ref[h : 2 * h, :] = mul(left, right, TN)
-        gram_ref[2 * h :, :] = mul(right, right, TN)
+        gram_ref[:h, :] = mul3(left, left, TN)
+        gram_ref[h : 2 * h, :] = mul3(left, right, TN)
+        gram_ref[2 * h :, :] = mul3(right, right, TN)
         ia, ja, ka = place_ref[0], place_ref[1], place_ref[2]
         for p in range(n_c):
             masks = origin(p, ia_bits[::-1] + ja_bits)
@@ -242,7 +249,7 @@
             out_ref[span(s, i_step), :] = jnp.sum(inner * b_ref[...].reshape(1, j_dev, rank), axis=1)
             return 0
 
-        lax.fori_loop(0, steps, step, 0)
+        lax.fori_loop(0, steps, step, 0, unroll=2)
 
     y, parts_a = call(
         first_kernel,
@@ -259,7 +266,7 @@
         gram_ref[h:, :h] = packed_ref[h : 2 * h, :].T
         gram_ref[h:, h:] = packed_ref[2 * h :, :]
         b = b_ref[...]
-        m_ref[...] = gram_ref[...] * mul(b, b, TN)
+        m_ref[...] = gram_ref[...] * mul3(b, b, TN)
         invert_first(m_ref, half_ref, cross_ref)
 
     halves, cross, gram_c = call(
@@ -294,15 +301,15 @@
     other_a = swap(parts_a, *stages[-1])
 
     def solve_a_kernel(place_ref, one_ref, other_ref, inverse_ref, a_ref, own_ref, gram_ref, rows_ref, packed_ref):
-        a = mul(one_ref[...] + other_ref[...], inverse_ref[...])
+        a = mul3(one_ref[...] + other_ref[...], inverse_ref[...])
         a_ref[...] = a
         rows_ref[...] = a.reshape(n_a, a_rows, rank)
         own_ref[...] = rows_ref[place_ref[1] * n_ka + place_ref[2]]
         left, right = a[:, :h], a[:, h:]
-        middle = mul(left, right, TN)
-        packed_ref[0, :h, :] = mul(left, left, TN)
+        middle = mul3(left, right, TN)
+        packed_ref[0, :h, :] = mul3(left, left, TN)
         packed_ref[0, h:, :] = middle[: h // 2]
-        packed_ref[1, :h, :] = mul(right, right, TN)
+        packed_ref[1, :h, :] = mul3(right, right, TN)
         packed_ref[1, h:, :] = middle[h // 2 :]
         gram_ref[...] = packed_ref[place_ref[1] & 1]
 
@@ -391,7 +398,7 @@
     )
 
     def solve_b_kernel(place_ref, one_ref, other_ref, inverse_ref, b_ref, own_ref, rows_ref):
-        b = mul(one_ref[...] + other_ref[...], inverse_ref[...])
+        b = mul3(one_ref[...] + other_ref[...], inverse_ref[...])
         b_ref[...] = b
         rows_ref[...] = b.reshape(n_b, b_rows, rank)
         own_ref[...] = rows_ref[place_ref[0] * n_ka + place_ref[2]]
@@ -414,7 +421,7 @@
             more = lax.dot_general(turned_ref[:k_dev, span(s, depth)], low, NN, preferred_element_type=F32)
             return total + (both[:k_dev] + (both[k_dev:] + more))
 
-        out_ref[...] = lax.fori_loop(0, steps, step, jnp.zeros((k_dev, rank), F32))
+        out_ref[...] = lax.fori_loop(0, steps, step, jnp.zeros((k_dev, rank), F32), unroll=2)
 
     (parts_c,) = call(
         third_kernel,
@@ -430,7 +437,7 @@
 
     def invert_c_kernel(b_ref, gram_a_ref, inverse_ref, m_ref, half_ref, cross_ref):
         b = b_ref[...]
-        m_ref[...] = gram_a_ref[...] * mul(b, b, TN)
+        m_ref[...] = gram_a_ref[...] * mul3(b, b, TN)
         invert_first(m_ref, half_ref, cross_ref)
         invert_last(half_ref, cross_ref, inverse_ref)
 
@@ -444,7 +451,7 @@
     )
 
     def solve_c_kernel(sums_ref, inverse_ref, out_ref):
-        out_ref[...] = mul(tree(sums_ref[q] for q in range(n_c)), inverse_ref[...])
+        out_ref[...] = mul3(tree(sums_ref[q] for q in range(n_c)), inverse_ref[...])
 
     (new_c,) = call(solve_c_kernel, "solve_c", [sums_c, inverse_c], [((c_rows, rank), F32)])
     return (new_a[None], new_b[None], new_c[None])

time: 90 us -> 88.4 us (0.982)
  Pallas kernels: 52.5 us -> 50.2 us
    pallas_call x15, Pallas kernels: 52.5 us -> 50.2 us  [call(): pl.pallas_call(kernel, grid=grid, out_shape=[jax.ShapeDtypeStruct(shape,...]
  transfers between devices with their start and end apart: 21 -> 21, of which waited for: 9 -> 8; matrix products, arithmetic and copies ran while one was open for 0% -> 0% of each run, Pallas kernels for 54% -> 52%
where the time goes in v2:
time: 88.4 us; the launch traced here: 87.9 us
  Pallas kernels  50.2 us (57%)
  starting transfers between devices  26.9 us (30%)
  waiting for transfers between devices  9.66 us (11%)
  between operations  0.9 us (1%)
    pallas_call x15, Pallas kernels, call(): pl.pallas_call(kernel, grid=grid, out_shape=[jax.ShapeDtypeStruct(shape,...  50.2 us
    ppermute x20, starting transfers between devices, swap(): lax.ppermute(value, axis, [(rank, rank ^ distance) for rank in range(lax....  23.1 us
    ppermute x20, waiting for transfers between devices, swap(): lax.ppermute(value, axis, [(rank, rank ^ distance) for rank in range(lax....  9.31 us
    all_to_all x1, starting transfers between devices, on_device(): lax.all_to_all(parts_c.reshape(n_c, c_rows, rank), ('ia', 'ja'), split_ax...  3.76 us
  transfers between devices with their start and end apart: 21, of which 8 were waited for; matrix products, arithmetic and copies ran while one was open for 0% of the time, Pallas kernels for 52%

profile of v2, /device:TPU:0, one launch (start us, length us, event | category | flops | bytes accessed | tf_op | source)
XLA Modules:
  0.0 87.9 jit_solution(13701958425474346198)
XLA Ops:
  1.4 5.1 %collective-permute-start.2 = (f32[24,256]{1,0:T(8,128)S(1)}, f32[24,256]{1,0:T(8,128)S(1)}, u32[]{:S(2)}, u32[]{:S(2)}) collective-permute-start(f32[24,256]{1,0:T(8,128)S(1)} %pack.1), channel_id=1, source_target_pairs={{0,24},{8,16},{16,8},{24,0},{1,25},{9,17},{17,9},{25,1},{2,26},{10... | collective-permute-start | bytes 73736 | tf_op jit(solution)/shard_map/ppermute | solution.py:48
  7.1 3.6 %load.1 = (bf16[8192,256]{1,0:T(8,128)(2,1)S(1)}, bf16[8192,256]{1,0:T(8,128)(2,1)S(1)}) custom-call(f32[128,64,256]{2,1,0:T(8,128)} %t_ref.1), custom_call_target="tpu_custom_call" | custom-call | bytes 16777216 | tf_op jit(solution)/shard_map/load/pallas_call | solution.py:147
  11.2 1.5 %collective-permute-start.5 = (f32[32,256]{1,0:T(8,128)S(1)}, f32[32,256]{1,0:T(8,128)S(1)}, u32[]{:S(2)}, u32[]{:S(2)}) collective-permute-start(f32[32,256]{1,0:T(8,128)S(1)} %maximum_bitcast_fusion), channel_id=1, source_target_pairs={{0,1},{1,0},{2,3},{3,2},{4,5},{5,4},{6,7},{7,6},{8,9},{9,8},{10,11... | collective-permute-start | bytes 98312 | tf_op jit(solution)/shard_map/ppermute | solution.py:48
  12.8 1.6 %collective-permute-start.3 = (f32[64,256]{1,0:T(8,128)S(1)}, f32[64,256]{1,0:T(8,128)S(1)}, u32[]{:S(2)}, u32[]{:S(2)}) collective-permute-start(f32[64,256]{1,0:T(8,128)S(1)} %bitcast.16), channel_id=1, source_target_pairs={{0,4},{2,6},{4,0},{6,2},{1,5},{3,7},{5,1},{7,3},{8,12},{10,14},{12... | collective-permute-start | bytes 196616 | tf_op jit(solution)/shard_map/ppermute | solution.py:48
  15.2 1.9 %collective-permute-done.3 = f32[64,256]{1,0:T(8,128)S(1)} collective-permute-done((f32[64,256]{1,0:T(8,128)S(1)}, f32[64,256]{1,0:T(8,128)S(1)}, u32[]{:S(2)}, u32[]{:S(2)}) %collective-permute-start.3) | collective-permute-done | bytes 65568 | tf_op jit(solution)/shard_map/ppermute | solution.py:48
  17.3 1.6 %collective-permute-start.8 = (f32[128,256]{1,0:T(8,128)S(1)}, f32[128,256]{1,0:T(8,128)S(1)}, u32[]{:S(2)}, u32[]{:S(2)}) collective-permute-start(f32[128,256]{1,0:T(8,128)S(1)} %pad_maximum_fusion.4), channel_id=1, source_target_pairs={{0,4},{2,6},{4,0},{6,2},{1,5},{3,7},{5,1},{7,3},{8,12},{10,14},{12... | collective-permute-start | bytes 393224 | tf_op jit(solution)/shard_map/ppermute | solution.py:48
  20.5 4.0 %first.1 = (f32[128,64,256]{2,1,0:T(8,128)S(1)}, f32[128,256]{1,0:T(8,128)S(1)}) custom-call(bf16[8192,256]{1,0:T(8,128)(2,1)S(1)} %get-tuple-element.65.high_ref, bf16[8192,256]{1,0:T(8,128)(2,1)S(1)} %get-tuple-element.66.low_ref, bf16[768,256]{1,0:T(8,128)(2,1)S(1)} %get-tuple-element.49.tall_ref, f32[64,256]{1,0:T(8,128)S(1)} %get-tuple-element.50.b_ref), custom_call_target="tpu_custom_call" | custom-call | flops 3221225472 | bytes 16777216 | tf_op jit(solution)/shard_map/first/pallas_call | solution.py:147
  26.9 4.8 %invert_a_first.1 = (f32[2,128,128]{2,1,0:T(8,128)S(1)}, f32[128,128]{1,0:T(8,128)S(1)}, f32[256,256]{1,0:T(8,128)S(1)}) custom-call(f32[384,128]{1,0:T(8,128)S(1)} %add.21.packed_ref, f32[256,256]{1,0:T(8,128)S(1)} %pad_maximum_fusion.1.b_ref), custom_call_target="tpu_custom_call" | custom-call | flops 5000000000 | bytes 1048576 | tf_op jit(solution)/shard_map/invert_a_first/pallas_call | solution.py:147
  32.3 4.7 %invert_a_last.1.inverse_ref = f32[256,256]{1,0:T(8,128)S(1)} custom-call(f32[2,128,128]{2,1,0:T(8,128)S(1)} %get-tuple-element.56.half_in, f32[128,128]{1,0:T(8,128)S(1)} %get-tuple-element.57.cross_ref), custom_call_target="tpu_custom_call" | custom-call | flops 5000000000 | bytes 1048576 | tf_op jit(solution)/shard_map/invert_a_last/pallas_call | solution.py:147
  37.1 1.3 %collective-permute-done.11.other_ref = f32[128,256]{1,0:T(8,128)S(1)} collective-permute-done((f32[128,256]{1,0:T(8,128)S(1)}, f32[128,256]{1,0:T(8,128)S(1)}, u32[]{:S(2)}, u32[]{:S(2)}) %collective-permute-start.11) | collective-permute-done | bytes 131104 | tf_op jit(solution)/shard_map/ppermute | solution.py:48
  38.5 1.4 %solve_a.1 = (f32[128,256]{1,0:T(8,128)S(1)}, f32[16,256]{1,0:T(8,128)}, f32[192,128]{1,0:T(8,128)S(1)}) custom-call(s32[3]{0:T(128)S(1)} %pad_add_fusion.place_ref, f32[128,256]{1,0:T(8,128)S(1)} %add.23.one_ref, f32[128,256]{1,0:T(8,128)S(1)} %collective-permute-done.11.other_ref, f32[256,256]{1,0:T(8,128)S(1)} %invert_a_last.1.inverse_ref), custom_call_target="tpu_custom_call" | custom-call | bytes 1048576 | tf_op jit(solution)/shard_map/solve_a/pallas_call | solution.py:147
  39.9 2.0 %collective-permute-start.12 = (f32[192,128]{1,0:T(8,128)S(1)}, f32[192,128]{1,0:T(8,128)S(1)}, u32[]{:S(2)}, u32[]{:S(2)}) collective-permute-start(f32[192,128]{1,0:T(8,128)S(1)} %get-tuple-element.64), channel_id=1, source_target_pairs={{0,16},{8,24},{16,0},{24,8},{1,17},{9,25},{17,1},{25,9},{2,18},{10... | collective-permute-start | bytes 294920 | tf_op jit(solution)/shard_map/ppermute | solution.py:48
  42.8 1.6 %collective-permute-start.13 = (f32[64,256]{1,0:T(8,128)S(1)}, f32[64,256]{1,0:T(8,128)S(1)}, u32[]{:S(2)}, u32[]{:S(2)}) collective-permute-start(f32[64,256]{1,0:T(8,128)S(1)} %second.1), channel_id=1, source_target_pairs={{0,1},{1,0},{2,3},{3,2},{4,5},{5,4},{6,7},{7,6},{8,9},{9,8},{10,11... | collective-permute-start | bytes 196616 | tf_op jit(solution)/shard_map/ppermute | solution.py:48
  44.4 2.9 %turn.1.turned_ref = bf16[512,8192]{1,0:T(8,128)(2,1)S(1)} custom-call(bf16[8192,256]{1,0:T(8,128)(2,1)S(1)} %get-tuple-element.65.high_ref, bf16[8192,256]{1,0:T(8,128)(2,1)S(1)} %get-tuple-element.66.low_ref), custom_call_target="tpu_custom_call" | custom-call | bytes 16777216 | tf_op jit(solution)/shard_map/turn/pallas_call | solution.py:147
  47.8 1.6 %collective-permute-start.14 = (f32[192,128]{1,0:T(8,128)S(1)}, f32[192,128]{1,0:T(8,128)S(1)}, u32[]{:S(2)}, u32[]{:S(2)}) collective-permute-start(f32[192,128]{1,0:T(8,128)S(1)} %add.25), channel_id=1, source_target_pairs={{0,8},{8,0},{16,24},{24,16},{1,9},{9,1},{17,25},{25,17},{2,10},{10... | collective-permute-start | bytes 294920 | tf_op jit(solution)/shard_map/ppermute | solution.py:48
  49.4 3.1 %collective-permute-done.14 = f32[192,128]{1,0:T(8,128)S(1)} collective-permute-done((f32[192,128]{1,0:T(8,128)S(1)}, f32[192,128]{1,0:T(8,128)S(1)}, u32[]{:S(2)}, u32[]{:S(2)}) %collective-permute-start.14) | collective-permute-done | bytes 98336 | tf_op jit(solution)/shard_map/ppermute | solution.py:48
  52.5 1.9 %collective-permute-start.16 = (f32[64,256]{1,0:T(8,128)S(1)}, f32[64,256]{1,0:T(8,128)S(1)}, u32[]{:S(2)}, u32[]{:S(2)}) collective-permute-start(f32[64,256]{1,0:T(8,128)S(1)} %add.24), channel_id=1, source_target_pairs={{0,16},{8,24},{16,0},{24,8},{1,17},{9,25},{17,1},{25,9},{2,18},{10... | collective-permute-start | bytes 196616 | tf_op jit(solution)/shard_map/ppermute | solution.py:48
  54.5 5.2 %invert_b_first.1 = (f32[256,256]{1,0:T(8,128)S(1)}, f32[2,128,128]{2,1,0:T(8,128)S(1)}, f32[128,128]{1,0:T(8,128)S(1)}) custom-call(s32[3]{0:T(128)S(1)} %pad_add_fusion.place_ref, f32[192,128]{1,0:T(8,128)S(1)} %add.26.one_ref, f32[192,128]{1,0:T(8,128)S(1)} %collective-permute-done.15.other_ref, f32[256,256]{1,0:T(8,128)S(1)} %get-tuple-element.69.gram_c_ref), custom_call_target="tpu_custom_call" | custom-call | flops 5000000000 | bytes 1048576 | tf_op jit(solution)/shard_map/invert_b_first/pallas_call | solution.py:147
  59.7 1.8 %collective-permute-start.17 = (f32[64,256]{1,0:T(8,128)S(1)}, f32[64,256]{1,0:T(8,128)S(1)}, u32[]{:S(2)}, u32[]{:S(2)}) collective-permute-start(f32[64,256]{1,0:T(8,128)S(1)} %add.27.one_ref), channel_id=1, source_target_pairs={{0,8},{8,0},{16,24},{24,16},{1,9},{9,1},{17,25},{25,17},{2,10},{10... | collective-permute-start | bytes 196616 | tf_op jit(solution)/shard_map/ppermute | solution.py:48
  61.5 4.7 %invert_b_last.1.inverse_ref = f32[256,256]{1,0:T(8,128)S(1)} custom-call(f32[2,128,128]{2,1,0:T(8,128)S(1)} %get-tuple-element.73.half_in, f32[128,128]{1,0:T(8,128)S(1)} %get-tuple-element.74.cross_ref), custom_call_target="tpu_custom_call" | custom-call | flops 5000000000 | bytes 1048576 | tf_op jit(solution)/shard_map/invert_b_last/pallas_call | solution.py:147
  66.3 1.3 %solve_b.1 = (f32[64,256]{1,0:T(8,128)S(1)}, f32[8,256]{1,0:T(8,128)}) custom-call(s32[3]{0:T(128)S(1)} %pad_add_fusion.place_ref, f32[64,256]{1,0:T(8,128)S(1)} %add.27.one_ref, f32[64,256]{1,0:T(8,128)S(1)} %collective-permute-done.17.other_ref, f32[256,256]{1,0:T(8,128)S(1)} %invert_b_last.1.inverse_ref), custom_call_target="tpu_custom_call" | custom-call | bytes 1048576 | tf_op jit(solution)/shard_map/solve_b/pallas_call | solution.py:147
  68.7 4.8 %third.1 = f32[256,256]{1,0:T(8,128)} custom-call(bf16[512,8192]{1,0:T(8,128)(2,1)S(1)} %turn.1.turned_ref, f32[128,256]{1,0:T(8,128)S(1)} %get-tuple-element.62.a_ref, f32[64,256]{1,0:T(8,128)S(1)} %get-tuple-element.76.b_ref), custom_call_target="tpu_custom_call" | custom-call | flops 3221225472 | bytes 8388608 | tf_op jit(solution)/shard_map/third/pallas_call | solution.py:147
  73.6 3.8 %all-to-all-start = ((f32[16,16,256]{2,1,0:T(8,128)}), f32[16,16,256]{2,1,0:T(8,128)S(1)}, u32[]{:S(2)}, u32[]{:S(2)}) async-start(f32[16,16,256]{2,1,0:T(8,128)} %bitcast.11), calls=%async_computation | async-start | bytes 524288 | tf_op jit(solution)/shard_map/all_to_all | solution.py:436
  77.4 9.4 %invert_c.1.inverse_ref = f32[256,256]{1,0:T(8,128)S(1)} custom-call(f32[256,256]{1,0:T(8,128)S(1)} %pad_maximum_fusion.2.b_ref, f32[256,256]{1,0:T(8,128)S(1)} %get-tuple-element.80.gram_a_ref), custom_call_target="tpu_custom_call" | custom-call | flops 10000000000 | bytes 1048576 | tf_op jit(solution)/shard_map/invert_c/pallas_call | solution.py:147
  (51 shorter events, 11.4 us)
Async XLA Ops:
  1.4 9.4 %collective-permute-start.2 = (f32[24,256]{1,0:T(8,128)S(1)}, f32[24,256]{1,0:T(8,128)S(1)}, u32[]{:S(2)}, u32[]{:S(2)}) collective-permute-start(f32[24,256]{1,0:T(8,128)S(1)} %pack.1), channel_id=1, source_target_pairs={{0,24},{8,16},{16,8},{24,0},{1,25},{9,17},{17,9},{25,1},{2,26},{10... | collective-permute-start | bytes 73736 | tf_op jit(solution)/shard_map/ppermute | solution.py:48
  6.5 4.7 %collective-permute-start.1 = (f32[24,256]{1,0:T(8,128)S(1)}, f32[24,256]{1,0:T(8,128)S(1)}, u32[]{:S(2)}, u32[]{:S(2)}) collective-permute-start(f32[24,256]{1,0:T(8,128)S(1)} %pack.1), channel_id=1, source_target_pairs={{0,16},{8,24},{16,0},{24,8},{1,17},{9,25},{17,1},{25,9},{2,18},{10... | collective-permute-start | bytes 73736 | tf_op jit(solution)/shard_map/ppermute | solution.py:48
  6.5 4.7 %collective-permute-start = (f32[24,256]{1,0:T(8,128)S(1)}, f32[24,256]{1,0:T(8,128)S(1)}, u32[]{:S(2)}, u32[]{:S(2)}) collective-permute-start(f32[24,256]{1,0:T(8,128)S(1)} %pack.1), channel_id=1, source_target_pairs={{0,8},{8,0},{16,24},{24,16},{1,9},{9,1},{17,25},{25,17},{2,10},{10... | collective-permute-start | bytes 73736 | tf_op jit(solution)/shard_map/ppermute | solution.py:48
  11.2 3.9 %collective-permute-start.5 = (f32[32,256]{1,0:T(8,128)S(1)}, f32[32,256]{1,0:T(8,128)S(1)}, u32[]{:S(2)}, u32[]{:S(2)}) collective-permute-start(f32[32,256]{1,0:T(8,128)S(1)} %maximum_bitcast_fusion), channel_id=1, source_target_pairs={{0,1},{1,0},{2,3},{3,2},{4,5},{5,4},{6,7},{7,6},{8,9},{9,8},{10,11... | collective-permute-start | bytes 98312 | tf_op jit(solution)/shard_map/ppermute | solution.py:48
  12.8 4.3 %collective-permute-start.3 = (f32[64,256]{1,0:T(8,128)S(1)}, f32[64,256]{1,0:T(8,128)S(1)}, u32[]{:S(2)}, u32[]{:S(2)}) collective-permute-start(f32[64,256]{1,0:T(8,128)S(1)} %bitcast.16), channel_id=1, source_target_pairs={{0,4},{2,6},{4,0},{6,2},{1,5},{3,7},{5,1},{7,3},{8,12},{10,14},{12... | collective-permute-start | bytes 196616 | tf_op jit(solution)/shard_map/ppermute | solution.py:48
  15.1 2.1 %collective-permute-start.7 = (f32[64,256]{1,0:T(8,128)S(1)}, f32[64,256]{1,0:T(8,128)S(1)}, u32[]{:S(2)}, u32[]{:S(2)}) collective-permute-start(f32[64,256]{1,0:T(8,128)S(1)} %pad_maximum_fusion.7.b_ref), channel_id=1, source_target_pairs={{0,2},{2,0},{4,6},{6,4},{1,3},{3,1},{5,7},{7,5},{8,10},{10,8},{12,... | collective-permute-start | bytes 196616 | tf_op jit(solution)/shard_map/ppermute | solution.py:48
  17.1 1.7 %collective-permute-start.4 = (f32[128,256]{1,0:T(8,128)S(1)}, f32[128,256]{1,0:T(8,128)S(1)}, u32[]{:S(2)}, u32[]{:S(2)}) collective-permute-start(f32[128,256]{1,0:T(8,128)S(1)} %pad_maximum_fusion.3), channel_id=1, source_target_pairs={{0,2},{2,0},{4,6},{6,4},{1,3},{3,1},{5,7},{7,5},{8,10},{10,8},{12,... | collective-permute-start | bytes 393224 | tf_op jit(solution)/shard_map/ppermute | solution.py:48
  17.3 8.3 %collective-permute-start.8 = (f32[128,256]{1,0:T(8,128)S(1)}, f32[128,256]{1,0:T(8,128)S(1)}, u32[]{:S(2)}, u32[]{:S(2)}) collective-permute-start(f32[128,256]{1,0:T(8,128)S(1)} %pad_maximum_fusion.4), channel_id=1, source_target_pairs={{0,4},{2,6},{4,0},{6,2},{1,5},{3,7},{5,1},{7,3},{8,12},{10,14},{12... | collective-permute-start | bytes 393224 | tf_op jit(solution)/shard_map/ppermute | solution.py:48
  19.8 7.1 %collective-permute-start.6 = (f32[384,128]{1,0:T(8,128)S(1)}, f32[384,128]{1,0:T(8,128)S(1)}, u32[]{:S(2)}, u32[]{:S(2)}) collective-permute-start(f32[384,128]{1,0:T(8,128)S(1)} %get-tuple-element.52), channel_id=1, source_target_pairs={{0,1},{1,0},{2,3},{3,2},{4,5},{5,4},{6,7},{7,6},{8,9},{9,8},{10,11... | collective-permute-start | bytes 589832 | tf_op jit(solution)/shard_map/ppermute | solution.py:48
  24.5 7.2 %collective-permute-start.9 = (f32[128,256]{1,0:T(8,128)S(1)}, f32[128,256]{1,0:T(8,128)S(1)}, u32[]{:S(2)}, u32[]{:S(2)}) collective-permute-start(f32[128,256]{1,0:T(8,128)S(1)} %get-tuple-element.51), channel_id=1, source_target_pairs={{0,4},{2,6},{4,0},{6,2},{1,5},{3,7},{5,1},{7,3},{8,12},{10,14},{12... | collective-permute-start | bytes 393224 | tf_op jit(solution)/shard_map/ppermute | solution.py:48
  31.7 5.3 %collective-permute-start.10 = (f32[128,256]{1,0:T(8,128)S(1)}, f32[128,256]{1,0:T(8,128)S(1)}, u32[]{:S(2)}, u32[]{:S(2)}) collective-permute-start(f32[128,256]{1,0:T(8,128)S(1)} %add.22), channel_id=1, source_target_pairs={{0,1},{1,0},{2,3},{3,2},{4,5},{5,4},{6,7},{7,6},{8,9},{9,8},{10,11... | collective-permute-start | bytes 393224 | tf_op jit(solution)/shard_map/ppermute | solution.py:48
  37.1 1.4 %collective-permute-start.11 = (f32[128,256]{1,0:T(8,128)S(1)}, f32[128,256]{1,0:T(8,128)S(1)}, u32[]{:S(2)}, u32[]{:S(2)}) collective-permute-start(f32[128,256]{1,0:T(8,128)S(1)} %add.23.one_ref), channel_id=1, source_target_pairs={{0,2},{2,0},{4,6},{6,4},{1,3},{3,1},{5,7},{7,5},{8,10},{10,8},{12,... | collective-permute-start | bytes 393224 | tf_op jit(solution)/shard_map/ppermute | solution.py:48
  39.9 7.9 %collective-permute-start.12 = (f32[192,128]{1,0:T(8,128)S(1)}, f32[192,128]{1,0:T(8,128)S(1)}, u32[]{:S(2)}, u32[]{:S(2)}) collective-permute-start(f32[192,128]{1,0:T(8,128)S(1)} %get-tuple-element.64), channel_id=1, source_target_pairs={{0,16},{8,24},{16,0},{24,8},{1,17},{9,25},{17,1},{25,9},{2,18},{10... | collective-permute-start | bytes 294920 | tf_op jit(solution)/shard_map/ppermute | solution.py:48
  42.8 4.5 %collective-permute-start.13 = (f32[64,256]{1,0:T(8,128)S(1)}, f32[64,256]{1,0:T(8,128)S(1)}, u32[]{:S(2)}, u32[]{:S(2)}) collective-permute-start(f32[64,256]{1,0:T(8,128)S(1)} %second.1), channel_id=1, source_target_pairs={{0,1},{1,0},{2,3},{3,2},{4,5},{5,4},{6,7},{7,6},{8,9},{9,8},{10,11... | collective-permute-start | bytes 196616 | tf_op jit(solution)/shard_map/ppermute | solution.py:48
  47.8 4.7 %collective-permute-start.14 = (f32[192,128]{1,0:T(8,128)S(1)}, f32[192,128]{1,0:T(8,128)S(1)}, u32[]{:S(2)}, u32[]{:S(2)}) collective-permute-start(f32[192,128]{1,0:T(8,128)S(1)} %add.25), channel_id=1, source_target_pairs={{0,8},{8,0},{16,24},{24,16},{1,9},{9,1},{17,25},{25,17},{2,10},{10... | collective-permute-start | bytes 294920 | tf_op jit(solution)/shard_map/ppermute | solution.py:48
  52.5 2.0 %collective-permute-start.15 = (f32[192,128]{1,0:T(8,128)S(1)}, f32[192,128]{1,0:T(8,128)S(1)}, u32[]{:S(2)}, u32[]{:S(2)}) collective-permute-start(f32[192,128]{1,0:T(8,128)S(1)} %add.26.one_ref), channel_id=1, source_target_pairs={{0,2},{2,0},{4,6},{6,4},{1,3},{3,1},{5,7},{7,5},{8,10},{10,8},{12,... | collective-permute-start | bytes 294920 | tf_op jit(solution)/shard_map/ppermute | solution.py:48
  52.5 7.1 %collective-permute-start.16 = (f32[64,256]{1,0:T(8,128)S(1)}, f32[64,256]{1,0:T(8,128)S(1)}, u32[]{:S(2)}, u32[]{:S(2)}) collective-permute-start(f32[64,256]{1,0:T(8,128)S(1)} %add.24), channel_id=1, source_target_pairs={{0,16},{8,24},{16,0},{24,8},{1,17},{9,25},{17,1},{25,9},{2,18},{10... | collective-permute-start | bytes 196616 | tf_op jit(solution)/shard_map/ppermute | solution.py:48
  59.7 6.5 %collective-permute-start.17 = (f32[64,256]{1,0:T(8,128)S(1)}, f32[64,256]{1,0:T(8,128)S(1)}, u32[]{:S(2)}, u32[]{:S(2)}) collective-permute-start(f32[64,256]{1,0:T(8,128)S(1)} %add.27.one_ref), channel_id=1, source_target_pairs={{0,8},{8,0},{16,24},{24,16},{1,9},{9,1},{17,25},{25,17},{2,10},{10... | collective-permute-start | bytes 196616 | tf_op jit(solution)/shard_map/ppermute | solution.py:48
  67.6 5.9 %collective-permute-start.18 = (f32[64,256]{1,0:T(8,128)S(1)}, f32[64,256]{1,0:T(8,128)S(1)}, u32[]{:S(2)}, u32[]{:S(2)}) collective-permute-start(f32[64,256]{1,0:T(8,128)S(1)} %get-tuple-element.76.b_ref), channel_id=1, source_target_pairs={{0,4},{2,6},{4,0},{6,2},{1,5},{3,7},{5,1},{7,3},{8,12},{10,14},{12... | collective-permute-start | bytes 196616 | tf_op jit(solution)/shard_map/ppermute | solution.py:48
  73.5 3.9 %collective-permute-start.19 = (f32[128,256]{1,0:T(8,128)S(1)}, f32[128,256]{1,0:T(8,128)S(1)}, u32[]{:S(2)}, u32[]{:S(2)}) collective-permute-start(f32[128,256]{1,0:T(8,128)S(1)} %pad_maximum_fusion.5), channel_id=1, source_target_pairs={{0,2},{2,0},{4,6},{6,4},{1,3},{3,1},{5,7},{7,5},{8,10},{10,8},{12,... | collective-permute-start | bytes 393224 | tf_op jit(solution)/shard_map/ppermute | solution.py:48
  73.6 13.6 %all-to-all-start = ((f32[16,16,256]{2,1,0:T(8,128)}), f32[16,16,256]{2,1,0:T(8,128)S(1)}, u32[]{:S(2)}, u32[]{:S(2)}) async-start(f32[16,16,256]{2,1,0:T(8,128)} %bitcast.11), calls=%async_computation | async-start | bytes 524288 | tf_op jit(solution)/shard_map/all_to_all | solution.py:436
